TPU v7x, 512 devices: a whole 4x8x8 slice. The times are simulated.
512 devices in a mesh: req: 8 (over z), ctx: 4 (over x), exp: 16 (over y, core).
Axes of the slice: x: 4, y: 8, z: 8, core: 2. Of those that a mesh axis runs over, the one named last changes fastest.
Arguments:
- queries: bfloat16 [256, 6144], P(('req', 'exp')), may hold values from -25 to 25
- key_pages: bfloat16 [128, 12, 64, 1024], P(('req', 'exp'), 'ctx'), may hold values from -4 to 4
- value_pages: bfloat16 [128, 12, 64, 1024], P(('req', 'exp'), 'ctx'), may hold values from -15 to 15
- block_table: int32 [256, 8], P(('req', 'exp'), 'ctx'), may hold values from 0 to 2, as said below
- context_lengths: int32 [256], P(('req', 'exp')), may hold values from 2 to 512, as said below
- residual: bfloat16 [256, 6144], P(('req', 'exp')), may hold values from -4 to 4
- norm_gain: bfloat16 [6144], replicated, may hold values from 0.099609375 to 1.8984375
- gate_blocks: bfloat16 [16, 3072, 6144], P('exp', ('req', 'ctx')), may hold values from -0.078125 to 0.078125
- up_blocks: bfloat16 [16, 3072, 6144], P('exp', ('req', 'ctx')), may hold values from -0.078125 to 0.078125
- down_blocks: bfloat16 [16, 3072, 6144], P('exp', ('req', 'ctx')), may hold values from -0.078125 to 0.078125
- expert_routes: int32 [16, 16, 4], replicated, may hold values from 0 to 7, all different within a row; in each aligned block of 16 rows (0 to 15, 16 to 31, ..., all dimensions but the last counted through in order) at most 10 rows name the same one
- route_weights: float32 [16, 16, 4], replicated, may hold values from 0.05 to 0.5
- block_expert: int32 [16], replicated, may hold values from 0 to 7, as said below
Outputs:
- layer_out: bfloat16 [256, 6144], P(('req', 'exp'), 'ctx')
Inputs may be any that keep to these rules, and one draw needn't show every extreme that they name: `context_lengths`: each group holds 1 request longer than 256 positions and the others not longer. `block_table`: entries name slots of the request group's pool on the entry's context share; the live pages of one group on one share name distinct slots; entries of pages past a request's length name arbitrary slots. `expert_routes`: among the 16 rows of one index of the first dimension no expert is named more than 10 times; a row names 4 different experts. `block_expert`: each expert belongs to exactly two blocks.
All inputs are finite; a program needn't handle non-finite values.
Results may differ from a plain program's by a relative error of at most 0.015.
Values may be sent and summed in bfloat16 or wider, within the bound.
No kernel may reach another device: no remote copies, remote signals or barrier semaphores. Data moves between devices by JAX's collectives and lax.ppermute only.
A program may use at most 128 MiB of HBM per device.

v0:
```python
import jax
import jax.numpy as jnp
from jax import lax
from jax.sharding import PartitionSpec as P

HEADS = 48
KV_HEADS = 8
HEAD_DIM = 128
EXPERTS = 8
BLOCKS = 16


EPSILON = 1e-05
NEGATIVE = -1e30


def joined(part, axis, combine):
    gathered = jax.tree.map(lambda a: lax.all_gather(a, axis), part)

    def take(source):
        return jax.tree.map(lambda a: lax.dynamic_index_in_dim(a, source, 0, False), gathered)

    return lax.fori_loop(
        1, lax.axis_size(axis), lambda source, state: combine(state, take(source)), take(0)
    )


def merge_heads(first, second):
    mixes_a, score_a, weight_a = first
    mixes_b, score_b, weight_b = second
    top_score = jnp.maximum(score_a, score_b)
    scale_a = jnp.exp(score_a - top_score)
    scale_b = jnp.exp(score_b - top_score)
    return (
        mixes_a * scale_a[..., None] + mixes_b * scale_b[..., None],
        top_score,
        weight_a * scale_a + weight_b * scale_b,
    )


def on_device(
    queries,
    key_pages,
    value_pages,
    block_table,
    context_lengths,
    residual,
    norm_gain,
    gate_blocks,
    up_blocks,
    down_blocks,
    expert_routes,
    route_weights,
    block_expert,
):
    req_dev = queries.shape[0]
    model_width = queries.shape[1]
    n_ctx = lax.axis_size("ctx")
    n_req = lax.axis_size("req")
    n_exp = lax.axis_size("exp")
    ctx_index = lax.axis_index("ctx")
    exp_index = lax.axis_index("exp")
    group_size = HEADS // KV_HEADS
    page_span = block_table.shape[1]
    page_rows = key_pages.shape[2]
    col_share = model_width // n_ctx
    page_slots = block_table.reshape(-1)
    cached_keys = jnp.take(key_pages[0], page_slots, axis=0).reshape(
        req_dev, page_span * page_rows, KV_HEADS, HEAD_DIM
    )
    cached_values = jnp.take(value_pages[0], page_slots, axis=0).reshape(
        req_dev, page_span * page_rows, KV_HEADS, HEAD_DIM
    )
    logical = jnp.arange(page_span, dtype=jnp.int32)[:, None] * n_ctx + ctx_index
    positions = (logical * page_rows + jnp.arange(page_rows, dtype=jnp.int32)[None, :]).reshape(-1)
    is_live = (positions[None, :] < context_lengths[:, None])[:, None, None, :]
    grouped_query = queries.reshape(req_dev, KV_HEADS, group_size, HEAD_DIM)
    scores = jnp.einsum(
        "rkgd,rnkd->rkgn", grouped_query, cached_keys, preferred_element_type=jnp.float32
    ) * HEAD_DIM ** (-0.5)
    scores = jnp.where(is_live, scores, NEGATIVE)
    top_score = jnp.max(scores, axis=-1)
    weights = jnp.where(is_live, jnp.exp(scores - top_score[..., None]), 0.0)
    weight_sum = jnp.sum(weights, axis=-1)
    head_mixes = jnp.einsum(
        "rkgn,rnkd->rkgd",
        weights,
        cached_values.astype(jnp.float32),
        precision=lax.Precision.HIGHEST,
    )
    head_mixes, top_score, weight_sum = joined(
        (
            head_mixes.reshape(req_dev, HEADS, HEAD_DIM),
            top_score.reshape(req_dev, HEADS),
            weight_sum.reshape(req_dev, HEADS),
        ),
        "ctx",
        merge_heads,
    )
    attention = (head_mixes / weight_sum[..., None]).reshape(req_dev, model_width)
    stream = (residual.astype(jnp.float32) + attention).astype(jnp.bfloat16)
    stream_wide = stream.astype(jnp.float32)
    normed = (
        stream_wide
        * lax.rsqrt(jnp.mean(stream_wide * stream_wide, axis=-1, keepdims=True) + EPSILON)
        * norm_gain.astype(jnp.float32)
    ).astype(jnp.bfloat16)
    column_rows = lax.all_gather(normed, "req", axis=0, tiled=True)
    group_rows = column_rows.shape[0]
    capacity = 5 * group_rows // 8
    routes = lax.dynamic_index_in_dim(expert_routes, exp_index, 0, keepdims=False)
    route_gate = lax.dynamic_index_in_dim(route_weights, exp_index, 0, keepdims=False)
    expert_ids = jnp.arange(EXPERTS, dtype=jnp.int32)
    named_hot = (routes[:, :, None] == expert_ids).astype(jnp.float32)
    chosen = jnp.sum(named_hot, axis=1)
    gate_share = jnp.sum(route_gate[:, :, None] * named_hot, axis=1)
    slot_rank = jnp.cumsum(chosen, axis=0) - chosen
    owners = (block_expert[:, None] == expert_ids).astype(jnp.float32)
    block_chosen = jnp.dot(owners, chosen.T, precision=lax.Precision.HIGHEST)
    block_rank = jnp.dot(owners, slot_rank.T, precision=lax.Precision.HIGHEST)
    block_gate = jnp.dot(owners, gate_share.T, precision=lax.Precision.HIGHEST)
    slot_ids = jnp.arange(capacity, dtype=jnp.float32)
    selector = block_chosen[:, None, :] * (
        block_rank[:, None, :] == slot_ids[None, :, None]
    ).astype(jnp.float32)
    blocks_dev = gate_blocks.shape[0]
    outgoing = jnp.einsum(
        "bcr,rd->bcd",
        selector.astype(jnp.bfloat16),
        column_rows,
        preferred_element_type=jnp.float32,
    ).astype(jnp.bfloat16)
    outgoing = outgoing.reshape(n_exp, blocks_dev, capacity, model_width)
    received = lax.all_to_all(outgoing, "exp", split_axis=0, concat_axis=0, tiled=True)
    gate_act = jnp.einsum(
        "sqnd,qfd->sqnf", received, gate_blocks, preferred_element_type=jnp.float32
    )
    up_act = jnp.einsum("sqnd,qfd->sqnf", received, up_blocks, preferred_element_type=jnp.float32)
    active = (jax.nn.silu(gate_act) * up_act).astype(jnp.bfloat16)
    partial_out = jnp.einsum(
        "sqnf,qfd->sqnd", active, down_blocks, preferred_element_type=jnp.float32
    )
    returned = lax.all_to_all(partial_out, "exp", split_axis=0, concat_axis=0, tiled=True)
    pick_weight = (selector * block_gate[:, None, :]).reshape(BLOCKS, capacity, n_req, req_dev)
    partial_cols = returned.reshape(BLOCKS, capacity, n_ctx, col_share)
    home_terms = jnp.einsum(
        "bcrj,bcxd->rxjd", pick_weight, partial_cols, precision=lax.Precision.HIGHEST
    ).reshape(n_req * n_ctx, req_dev, col_share)
    expert_sum = lax.psum_scatter(home_terms, ("req", "ctx"), scatter_dimension=0, tiled=True)[0]
    own_cols = lax.dynamic_slice_in_dim(stream_wide, ctx_index * col_share, col_share, 1)
    return (own_cols + expert_sum).astype(jnp.bfloat16)


def solution(mesh):
    in_specs = (
        P(("req", "exp"), None),
        P(("req", "exp"), "ctx", None, None),
        P(("req", "exp"), "ctx", None, None),
        P(("req", "exp"), "ctx"),
        P(("req", "exp")),
        P(("req", "exp"), None),
        P(),
        P("exp", ("req", "ctx"), None),
        P("exp", ("req", "ctx"), None),
        P("exp", ("req", "ctx"), None),
        P(),
        P(),
        P(),
    )
    out_specs = P(("req", "exp"), "ctx")
    return jax.shard_map(
        on_device, mesh=mesh, in_specs=in_specs, out_specs=out_specs, check_vma=False
    )
```

profile of v0, /device:TPU:8, one launch (start us, length us, event | category | flops | bytes accessed | tf_op | source)
XLA Modules:
  0.0 454.7 jit_solution(3458375260389434618)
XLA Ops:
  6.5 0.9 reshape.121
  7.4 1.6 gather_fusion
  9.0 1.6 gather_fusion.1
  10.6 0.2 broadcast_select_fusion.1
  10.8 0.1 copy.107
  11.0 0.1 add.128
  11.1 0.1 copy.108
  11.3 0.1 broadcast_compare_fusion
  11.3 0.5 fusion.95
  11.8 0.1 all_gather_reshape.10
  11.9 0.2 fusion.60
  12.1 0.6 fusion.49
  12.7 12.5 %all_gather.12 = f32[4,2,48,128]{3,2,1,0:T(8,128)S(1)} all-gather(f32[1,2,48,128]{3,2,1,0:T(8,128)S(1)} %copy.86), channel_id=1, replica_groups=mesh['req'=8,'ctx'=4,'exp'=16] {'ctx'}, dimensions={0}, use_global_device_ids=true | all-gather | bytes 245760 | tf_op jit(solution)/shard_map/all_gather | solution.py:18
  25.2 0.1 all_gather_reshape.11
  25.3 9.4 %all_gather.14 = f32[4,2,48]{2,1,0:T(2,128)S(1)} all-gather(f32[1,2,48]{2,1,0:T(2,128)S(1)} %all_gather_reshape.11), channel_id=1, replica_groups=mesh['req'=8,'ctx'=4,'exp'=16] {'ctx'}, dimensions={0}, use_global_device_ids=true | all-gather | bytes 1920 | tf_op jit(solution)/shard_map/all_gather | solution.py:18
  34.6 7.0 %all_gather.13 = f32[4,2,48]{2,1,0:T(2,128)S(1)} all-gather(f32[1,2,48]{2,1,0:T(2,128)S(1)} %all_gather_reshape.10), channel_id=1, replica_groups=mesh['req'=8,'ctx'=4,'exp'=16] {'ctx'}, dimensions={0}, use_global_device_ids=true | all-gather | bytes 1920 | tf_op jit(solution)/shard_map/all_gather | solution.py:18
  41.6 0.4 while.19
  41.6 0.1 fusion.102
  41.8 0.1 fusion.102
  41.9 0.1 fusion.102
  42.1 0.1 divide_bitcast_fusion
  42.2 0.2 multiply_reduce_fusion
  42.4 0.1 fusion.74
  42.5 31.0 %all-gather = bf16[8,2,6144]{2,1,0:T(2,128)(2,1)S(1)} all-gather(bf16[1,2,6144]{2,1,0:T(2,128)(2,1)S(1)} %fusion.74), channel_id=1, replica_groups=mesh['req'=8,'ctx'=4,'exp'=16] {'req'}, dimensions={0}, use_global_device_ids=true | all-gather | bytes 221184 | tf_op jit(solution)/shard_map/all_gather | solution.py:108
  73.5 0.1 reshape.158
  73.6 0.7 dynamic-slice_bitcast_fusion.1
  74.3 0.7 dynamic-slice_bitcast_fusion.2
  75.0 0.1 copy.87
  75.0 0.2 fusion.82
  75.3 0.2 fusion.79
  75.4 0.6 fusion.3
  76.1 1.2 copy.89
  77.3 78.0 %all_to_all.10 = bf16[16,1,10,6144]{3,2,1,0:T(8,128)(2,1)S(1)} all-to-all(bf16[16,1,10,6144]{3,2,1,0:T(8,128)(2,1)S(1)} %copy.89), channel_id=1, replica_groups=mesh['req'=8,'ctx'=4,'exp'=16] {'exp'}, dimensions={0} | all-to-all | bytes 3932160 | tf_op jit(solution)/shard_map/all_to_all | solution.py:134
  155.4 1.7 copy-done.1
  157.0 1.3 fusion.18
  158.4 6.2 %convolution_bitcast_fusion = f32[16,1,10,6144]{3,0,2,1:T(8,128)} fusion(bf16[1,96,6144]{2,1,0:T(8,128)(2,1)S(1)} %copy-done, bf16[1,96,6144]{2,1,0:T(8,128)(2,1)S(1)} %copy-done.2, bf16[16,1,10,6144]{3,2,1,0:T(8,128)(2,1)} %copy-done.1, f32[16,1,10,96]{3,0,2,1:T(8,128)S(1)} %fusion.18), kind=kOutput, calls=%fused_computation.11 | convolution fusion | flops 377579520 | bytes 8318976 | tf_op jit(solution)/shard_map/sqnf,qfd->sqnd/dot_general | solution.py:140
  164.5 8.1 %copy.91 = f32[16,1,10,6144]{3,1,2,0:T(1,128)} copy(f32[16,1,10,6144]{3,0,2,1:T(8,128)} %convolution_bitcast_fusion) | data formatting | bytes 7864320 | tf_op jit(solution)/shard_map/sqnf,qfd->sqnd/transpose | solution.py:140
  172.7 6.0 %all-to-all-start.1 = ((f32[16,1,10,6144]{3,1,2,0:T(1,128)}), f32[16,1,10,6144]{3,1,2,0:T(1,128)}, u32[]{:S(2)}, u32[]{:S(2)}) async-start(f32[16,1,10,6144]{3,1,2,0:T(1,128)} %copy.91), calls=%async_computation.1 | async-start | bytes 7864320 | tf_op jit(solution)/shard_map/all_to_all | solution.py:143
  178.7 0.3 all-reduce.3.cloned.1.call-start
  179.2 0.1 fusion.77
  179.3 86.3 %all-to-all-done.1 = f32[16,1,10,6144]{3,1,2,0:T(1,128)} async-done(((f32[16,1,10,6144]{3,1,2,0:T(1,128)}), f32[16,1,10,6144]{3,1,2,0:T(1,128)}, u32[]{:S(2)}, u32[]{:S(2)}) %all-to-all-start.1) | async-done | bytes 3932192 | tf_op jit(solution)/shard_map/all_to_all | solution.py:143
  265.6 13.3 %reduce = f32[16,10,6144]{2,1,0:T(8,128)} reduce(f32[16,1,10,6144]{3,1,2,0:T(1,128)} %all-to-all-done.1, f32[]{:T(128)} %constant.123), dimensions={1}, to_apply=%all_to_all.7.reduce_sub_computation | reduce | bytes 7864324 | tf_op jit(solution)/shard_map/all_to_all | solution.py:143
  278.8 6.5 %reshape.167 = f32[16,10,4,1536]{3,2,1,0:T(4,128)} reshape(f32[16,10,6144]{2,1,0:T(8,128)} %reduce) | data formatting | bytes 7864320 | tf_op jit(solution)/shard_map/reshape | solution.py:145
  285.3 6.3 %fusion.6 = f32[8,4,2,1536]{3,0,2,1:T(8,128)S(1)} fusion(f32[16,10,4,1536,1]{3,2,1,0,4:T(4,128)} %bitcast.152, f32[16,8,2]{0,1,2:T(8,128)S(1)} %fusion.77, f32[16,8,2]{0,1,2:T(8,128)S(1)} %copy.96, f32[16,8,2]{0,1,2:T(8,128)S(1)} %copy.94), kind=kOutput, calls=%fused_computation.16 | convolution fusion | flops 188751360 | bytes 4328448 | tf_op jit(solution)/shard_map/bcrj,bcxd->rxjd/dot_general | solution.py:146
  291.6 1.1 copy.100
  292.7 1.3 dynamic-slice
  294.1 151.9 %all-reduce.3.cloned.1.call-done = f32[32,2,1536]{2,1,0:T(2,128)} async-done(((f32[32,2,1536]{2,1,0:T(2,128)}), f32[32,2,1536]{2,1,0:T(2,128)}) %all-reduce.3.cloned.1.call-update) | async-done | bytes 393232
  446.0 1.9 fusion.76
  (41 shorter events, 0.6 us)
Async XLA Ops:
  6.5 151.8 %copy-start = (bf16[1,96,6144]{2,1,0:T(8,128)(2,1)S(1)}, bf16[1,96,6144]{2,1,0:T(8,128)(2,1)}, u32[]{:S(2)}) copy-start(bf16[1,96,6144]{2,1,0:T(8,128)(2,1)} %param.26) | copy-start | bytes 3538948
  9.0 2.1 copy-start.3
  10.6 0.7 copy-start.8
  11.1 31.1 %copy-start.4 = (bf16[2,6144]{1,0:T(2,128)(2,1)S(1)}, bf16[2,6144]{1,0:T(2,128)(2,1)}, u32[]{:S(2)}) copy-start(bf16[2,6144]{1,0:T(2,128)(2,1)} %param.22) | copy-start | bytes 73732
  11.3 31.1 %copy-start.5 = (bf16[6144]{0:T(1024)(128)(2,1)S(1)}, bf16[6144]{0:T(1024)(128)(2,1)}, u32[]{:S(2)}) copy-start(bf16[6144]{0:T(1024)(128)(2,1)} %param.23) | copy-start | bytes 36868
  11.3 63.7 %copy-start.6 = (s32[16]{0:T(128)S(1)}, s32[16]{0:T(128)}, u32[]{:S(2)}) copy-start(s32[16]{0:T(128)} %param.29) | copy-start | bytes 196
  77.3 79.7 %copy-start.7 = (bf16[1,96,6144]{2,1,0:T(8,128)(2,1)S(1)}, bf16[1,96,6144]{2,1,0:T(8,128)(2,1)}, u32[]{:S(2)}) copy-start(bf16[1,96,6144]{2,1,0:T(8,128)(2,1)} %param.24) | copy-start | bytes 3538948
  155.4 1.7 copy-start.1
  157.0 1.3 copy-start.2
  172.7 92.9 %all-to-all-start.1 = ((f32[16,1,10,6144]{3,1,2,0:T(1,128)}), f32[16,1,10,6144]{3,1,2,0:T(1,128)}, u32[]{:S(2)}, u32[]{:S(2)}) async-start(f32[16,1,10,6144]{3,1,2,0:T(1,128)} %copy.91), calls=%async_computation.1 | async-start | bytes 7864320 | tf_op jit(solution)/shard_map/all_to_all | solution.py:143
  178.7 267.3 %all-reduce.3.cloned.1.call-start = ((), (), s32[]{:S(2)}) async-start(), calls=%async_computation.2 | async-start | bytes 786432
Sparse Core Ops, SparseCore 0:
  292.8 153.0 all-reduce.2
where the time goes:
time: 455 us
  waiting for transfers between devices  238 us (52%)
  blocking collectives  138 us (30%)
  local copies, waits for them, and re-layouts  26.3 us (6%)
  other arithmetic  16.5 us (4%)
  matrix products  15.9 us (3%)
  between operations  13.6 us (3%)
  starting transfers between devices  6.3 us (1%)
    unnamed x2, waiting for transfers between devices  152 us
    all_to_all x1, waiting for transfers between devices, on_device(): lax.all_to_all(partial_out, 'exp', split_axis=0, concat_axis=0, tiled=True)  86.3 us
    all_to_all x1, blocking collectives, on_device(): lax.all_to_all(outgoing, 'exp', split_axis=0, concat_axis=0, tiled=True)  78 us
    all_gather x1, blocking collectives, on_device(): column_rows = lax.all_gather(normed, 'req', axis=0, tiled=True)  31 us
    all_gather x3, blocking collectives, joined(): gathered = jax.tree.map(lambda a: lax.all_gather(a, axis), part)  28.8 us
    all_to_all x1, other arithmetic, on_device(): lax.all_to_all(partial_out, 'exp', split_axis=0, concat_axis=0, tiled=True)  13.3 us
  transfers between devices with their start and end apart: 2, of which 2 were waited for; matrix products, arithmetic and copies ran while one was open for 0% of the time, Pallas kernels for 0%

commit v1 on v0

v1 whole, which is shorter than its diff:
```python
import functools

import jax
import jax.numpy as jnp
import numpy as np
from jax import lax
from jax.experimental import pallas as pl
from jax.experimental.pallas import tpu as pltpu
from jax.sharding import PartitionSpec as P

HEADS = 48
KV_HEADS = 8
HEAD_DIM = 128
GROUP = HEADS // KV_HEADS
EPSILON = 1e-05
NEGATIVE = -1e30
ROWS = 16
LANES = 128
AXES = ("req", "ctx", "exp")
F32 = jnp.float32
BF16 = jnp.bfloat16


def exchange_groups(n_req, n_ctx, n_exp):
    cols = n_exp // 2

    def device(z, x, y, core):
        z, x, y = (z + core) % n_req, (x + core) % n_ctx, (y + core) % cols
        return (z * n_ctx + x) * n_exp + y * 2 + core

    near = [
        [
            device(2 * zh + zl, 2 * xh + xl, 2 * yh + yl, core)
            for xl in (0, 1)
            for zl in (0, 1)
            for yl in (0, 1)
        ]
        for core in (0, 1)
        for xh in range(n_ctx // 2)
        for zh in range(n_req // 2)
        for yh in range(cols // 2)
    ]
    far = [
        [
            device(2 * zh + zl, 2 * xh + xl, 2 * yh + yl, core)
            for xh in range(n_ctx // 2)
            for zh in range(n_req // 2)
            for yh in range(cols // 2)
        ]
        for core in (0, 1)
        for xl in (0, 1)
        for zl in (0, 1)
        for yl in (0, 1)
    ]
    return near, far


def attention_kernel(n_ctx, table, lengths, place, q_ref, k_ref, v_ref, out_ref, heads):
    requests, slots, page_rows = q_ref.shape[0], k_ref.shape[1], k_ref.shape[2]
    span = table.shape[1]
    positions = slots * page_rows
    heads[...] = jnp.zeros_like(heads)
    queries = q_ref[...].astype(F32)
    for r in range(requests):
        for h in range(HEADS):
            row = (h // GROUP) * ROWS + r * GROUP + h % GROUP
            heads[row : row + 1, :] = queries[r : r + 1, h * HEAD_DIM : (h + 1) * HEAD_DIM]
    at = lax.broadcasted_iota(jnp.int32, (ROWS, positions), 1)
    row_id = lax.broadcasted_iota(jnp.int32, (ROWS, positions), 0)
    slot, offset = at // page_rows, at % page_rows
    live = None
    for r in range(requests):
        seen = None
        for s in range(span):
            position = (s * n_ctx + place[0]) * page_rows + offset
            here = (slot == table[r, s]) & (position < lengths[r])
            seen = here if seen is None else seen | here
        live = seen if live is None else jnp.where(row_id < r * GROUP, live.astype(jnp.int32), seen.astype(jnp.int32)) > 0
    out_row = lax.broadcasted_iota(jnp.int32, (ROWS, LANES), 0)
    diagonal = out_row == lax.broadcasted_iota(jnp.int32, (ROWS, LANES), 1)
    keys = k_ref[0].reshape(positions, KV_HEADS * HEAD_DIM)
    values = v_ref[0].reshape(positions, KV_HEADS * HEAD_DIM)
    for k in range(KV_HEADS):
        lanes = slice(k * HEAD_DIM, (k + 1) * HEAD_DIM)
        query = heads[k * ROWS : (k + 1) * ROWS, :].astype(BF16)
        scores = lax.dot_general(
            query, keys[:, lanes], (((1,), (1,)), ((), ())), preferred_element_type=F32
        ) * HEAD_DIM ** (-0.5)
        scores = jnp.where(live, scores, NEGATIVE)
        top = jnp.max(scores, axis=1, keepdims=True)
        weights = jnp.where(live, jnp.exp(scores - top), 0.0)
        total = jnp.sum(weights, axis=1, keepdims=True)
        high = weights.astype(BF16)
        low = (weights - high.astype(F32)).astype(BF16)
        mixes = jnp.dot(
            jnp.concatenate([high, low], axis=0), values[:, lanes], preferred_element_type=F32
        )
        mixes = mixes[:ROWS] + mixes[ROWS:]
        top_row = jnp.sum(jnp.where(diagonal, top, 0.0), axis=0, keepdims=True)
        total_row = jnp.sum(jnp.where(diagonal, total, 0.0), axis=0, keepdims=True)
        used = requests * GROUP
        out_ref[k] = jnp.where(
            out_row < used, mixes, jnp.where(out_row == used, top_row, total_row)
        )


def attention_parts(queries, key_pages, value_pages, block_table, lengths, place, n_ctx):
    smem = pl.BlockSpec(memory_space=pltpu.SMEM)
    vmem = pl.BlockSpec(memory_space=pltpu.VMEM)
    return pl.pallas_call(
        functools.partial(attention_kernel, n_ctx),
        out_shape=jax.ShapeDtypeStruct((KV_HEADS, ROWS, HEAD_DIM), F32),
        in_specs=[smem, smem, smem, vmem, vmem, vmem],
        out_specs=vmem,
        scratch_shapes=[pltpu.VMEM((KV_HEADS * ROWS, HEAD_DIM), F32)],
        name="attention_parts",
    )(block_table, lengths, place, queries, key_pages, value_pages)


def merge_kernel(place, parts_ref, residual_ref, gain_ref, piece_ref, stream_ref, merged):
    n_src, kv_here = parts_ref.shape[0], parts_ref.shape[1]
    requests, width = stream_ref.shape
    used = requests * GROUP
    diagonal = lax.broadcasted_iota(jnp.int32, (ROWS, LANES), 0) == lax.broadcasted_iota(
        jnp.int32, (ROWS, LANES), 1
    )

    def column(row):
        return jnp.sum(jnp.where(diagonal, row, 0.0), axis=1, keepdims=True)

    for k in range(kv_here):
        tops = [column(parts_ref[s, k, used : used + 1, :]) for s in range(n_src)]
        totals = [column(parts_ref[s, k, used + 1 : used + 2, :]) for s in range(n_src)]
        top = functools.reduce(jnp.maximum, tops)
        scales = [jnp.exp(t - top) for t in tops]
        mixes = sum(parts_ref[s, k] * scales[s] for s in range(n_src))
        total = sum(totals[s] * scales[s] for s in range(n_src))
        mixes = mixes / total
        for r in range(requests):
            for g in range(GROUP):
                at = (k * GROUP + g) * HEAD_DIM
                merged[r : r + 1, at : at + HEAD_DIM] = mixes[r * GROUP + g : r * GROUP + g + 1, :]
    columns = pl.ds(pl.multiple_of(place[0] * width, width), width)
    stream = (residual_ref[:, columns].astype(F32) + merged[...]).astype(BF16)
    stream_ref[...] = stream
    wide = stream.astype(F32)
    piece_ref[:, :width] = (wide * gain_ref[:, columns].astype(F32)).astype(BF16)
    square = jnp.sum(wide * wide, axis=1, keepdims=True)
    first = square.astype(BF16).astype(F32)
    second = (square - first).astype(BF16).astype(F32)
    third = square - first - second
    lane = lax.broadcasted_iota(jnp.int32, (requests, LANES), 1)
    spread = jnp.where(
        lane == 0, first, jnp.where(lane == 1, second, jnp.where(lane == 2, third, 0.0))
    )
    piece_ref[:, width:] = spread.astype(BF16)


def merge_parts(parts, residual, gain, place, width):
    requests = residual.shape[0]
    smem = pl.BlockSpec(memory_space=pltpu.SMEM)
    vmem = pl.BlockSpec(memory_space=pltpu.VMEM)
    return pl.pallas_call(
        merge_kernel,
        out_shape=(
            jax.ShapeDtypeStruct((requests, width + LANES), BF16),
            jax.ShapeDtypeStruct((requests, width), BF16),
        ),
        in_specs=[smem, vmem, vmem, vmem],
        out_specs=(vmem, vmem),
        scratch_shapes=[pltpu.VMEM((requests, width), F32)],
        name="merge_parts",
    )(place, parts, residual, gain)


def expert_kernel(
    model_width,
    core,
    tokens_ref,
    shares_ref,
    gate_a,
    gate_b,
    up_a,
    up_b,
    down_a,
    down_b,
    out_ref,
    gates,
    ups,
    squares,
    active,
):
    step = pl.program_id(0)
    chunks = pl.num_programs(0) // 2
    rows, width = gates.shape[1], gate_a.shape[2]

    @pl.when(step == 0)
    def _():
        gates[...] = jnp.zeros_like(gates)
        ups[...] = jnp.zeros_like(ups)
        squares[...] = jnp.zeros_like(squares)

    @pl.when(step < chunks)
    def _():
        tokens = tokens_ref[0, :, 0].reshape(rows, width + LANES)
        squares[...] += tokens[:, width:].astype(F32)
        tokens = tokens[:, :width]
        for b, (gate, up) in enumerate(((gate_a, up_a), (gate_b, up_b))):
            contract = (((1,), (1,)), ((), ()))
            gates[b] += lax.dot_general(tokens, gate[0], contract, preferred_element_type=F32)
            ups[b] += lax.dot_general(tokens, up[0], contract, preferred_element_type=F32)

    @pl.when(step == chunks - 1)
    def _():
        square = jnp.sum(squares[...], axis=1, keepdims=True)
        scale = lax.rsqrt(square / model_width + EPSILON)
        for b in range(2):
            gate, up = gates[b] * scale, ups[b] * scale
            silu = gate / (1.0 + jnp.exp(-gate))
            active[b] = (silu * up * shares_ref[:, b : b + 1]).astype(BF16)

    @pl.when(step >= chunks)
    def _():
        total = jnp.dot(active[0], down_a[0], preferred_element_type=F32) + jnp.dot(
            active[1], down_b[0], preferred_element_type=F32
        )
        out_ref[0, :, 0] = total.astype(BF16).reshape(out_ref.shape[1], out_ref.shape[3], width)


def expert_partials(tokens, shares, weights, core, n_ctx):
    n_xl, quarters, n_xh, far_rows, padded = tokens.shape
    width = padded - LANES
    rows = quarters * far_rows
    hidden = weights[0].shape[1]

    def first(i):
        return jnp.minimum(i, n_ctx - 1)

    def second(i):
        return jnp.maximum(i - n_ctx, 0)

    def owner(step, core):
        return lax.rem((step % n_xh) * 2 + step // n_xh + core[0], n_ctx)

    def token_block(i, core):
        return (first(i) // n_xh, 0, first(i) % n_xh, 0, 0)

    def wide_block(i, core):
        return (0, 0, owner(first(i), core))

    def down_block(i, core):
        return (0, 0, owner(second(i), core))

    def out_block(i, core):
        return (second(i) // n_xh, 0, second(i) % n_xh, 0, 0)

    weight_shape = (1, hidden, width)
    flops = 6 * rows * 2 * hidden * width * n_ctx
    return pl.pallas_call(
        functools.partial(expert_kernel, float(width * n_ctx)),
        out_shape=jax.ShapeDtypeStruct((n_xl, quarters, n_xh, far_rows, width), BF16),
        grid_spec=pltpu.PrefetchScalarGridSpec(
            num_scalar_prefetch=1,
            grid=(2 * n_ctx,),
            in_specs=[
                pl.BlockSpec((1, quarters, 1, far_rows, padded), token_block),
                pl.BlockSpec((rows, 2), lambda i, core: (0, 0)),
            ]
            + [pl.BlockSpec(weight_shape, wide_block)] * 4
            + [pl.BlockSpec(weight_shape, down_block)] * 2,
            out_specs=pl.BlockSpec((1, quarters, 1, far_rows, width), out_block),
            scratch_shapes=[
                pltpu.VMEM((2, rows, hidden), F32),
                pltpu.VMEM((2, rows, hidden), F32),
                pltpu.VMEM((rows, LANES), F32),
                pltpu.VMEM((2, rows, hidden), BF16),
            ],
        ),
        cost_estimate=pl.CostEstimate(
            flops=flops, bytes_accessed=12 * hidden * width * n_ctx, transcendentals=0
        ),
        name="expert_partials",
    )(core, tokens, shares, *weights)


def row_shares(expert_routes, route_weights, block_expert, exp_index, core, n_req):
    cols = expert_routes.shape[0] // 2
    requests = expert_routes.shape[1] // n_req

    def own(routes):
        return lax.dynamic_index_in_dim(
            routes.reshape((cols, 2) + routes.shape[1:]), core, 1, keepdims=False
        )

    routes, gate = own(expert_routes), own(route_weights)
    blocks = jnp.stack([block_expert[exp_index], block_expert[exp_index ^ 1]])
    shares = jnp.sum(
        jnp.where(routes[..., None] == blocks, gate[..., None], 0.0), axis=2
    ).reshape(cols, n_req, requests, 2)
    shares = jnp.where(core > 0, jnp.roll(shares, (-1, -1), (0, 1)), shares)
    shares = shares.reshape(cols // 2, 2, n_req // 2, 2, requests, 2)
    return shares.transpose(3, 1, 2, 0, 4, 5).reshape(-1, 2)


def on_device(
    groups,
    queries,
    key_pages,
    value_pages,
    block_table,
    context_lengths,
    residual,
    norm_gain,
    gate_blocks,
    up_blocks,
    down_blocks,
    expert_routes,
    route_weights,
    block_expert,
):
    near, far = groups
    n_req, n_ctx, n_exp = (lax.axis_size(a) for a in AXES)
    requests, model_width = queries.shape
    width = model_width // n_ctx
    place = lax.axis_index("ctx")
    exp_index = lax.axis_index("exp")
    core = exp_index % 2
    n_near, n_far = len(near[0]), len(far[0])
    far_rows = n_far // 2 * requests

    swap = [(i, i ^ 1) for i in range(n_exp)]
    gate_other, up_other, down_other = (
        lax.ppermute(w, "exp", swap) for w in (gate_blocks, up_blocks, down_blocks)
    )
    shares = row_shares(expert_routes, route_weights, block_expert, exp_index, core, n_req)

    parts = attention_parts(
        queries, key_pages, value_pages, block_table, context_lengths, place[None], n_ctx
    )
    parts = parts.reshape(n_ctx, KV_HEADS // n_ctx, ROWS, HEAD_DIM)
    parts = lax.all_to_all(parts, "ctx", 0, 0, tiled=True)
    piece, stream = merge_parts(
        parts, residual, norm_gain.reshape(1, model_width), place[None], width
    )

    def exchange(x, groups):
        return lax.all_to_all(x, AXES, 0, 0, axis_index_groups=groups, tiled=True)

    tokens = exchange(jnp.broadcast_to(piece, (n_far,) + piece.shape), far)
    tokens = tokens.reshape(2, far_rows, width + LANES)
    tokens = exchange(jnp.broadcast_to(tokens, (n_near,) + tokens.shape), near)
    tokens = tokens.reshape(2, n_near // 2, 2, far_rows, width + LANES)
    partials = expert_partials(
        tokens,
        shares,
        (gate_blocks, gate_other, up_blocks, up_other, down_blocks, down_other),
        core[None],
        n_ctx,
    )
    partials = exchange(partials.reshape(n_near, 2, far_rows, width), near)
    partials = jnp.sum(partials.astype(F32), axis=0).astype(BF16)
    partials = exchange(partials.reshape(n_far, requests, width), far)
    expert_sum = jnp.sum(partials.astype(F32), axis=0)
    return (stream.astype(F32) + expert_sum).astype(BF16)


def solution(mesh):
    in_specs = (
        P(("req", "exp"), None),
        P(("req", "exp"), "ctx", None, None),
        P(("req", "exp"), "ctx", None, None),
        P(("req", "exp"), "ctx"),
        P(("req", "exp")),
        P(("req", "exp"), None),
        P(),
        P("exp", ("req", "ctx"), None),
        P("exp", ("req", "ctx"), None),
        P("exp", ("req", "ctx"), None),
        P(),
        P(),
        P(),
    )
    out_specs = P(("req", "exp"), "ctx")
    groups = exchange_groups(*(mesh.shape[a] for a in AXES))
    return jax.shard_map(
        functools.partial(on_device, groups),
        mesh=mesh,
        in_specs=in_specs,
        out_specs=out_specs,
        check_vma=False,
    )
```

time: 455 us -> 119 us (0.26)
  the two profiles are of different devices: /device:TPU:8 before, /device:TPU:75 now
where the time goes in v1:
time: 119 us; the launch traced here: 118 us
  blocking collectives  71 us (60%)
  starting transfers between devices  19.4 us (16%)
  Pallas kernels  14.7 us (12%)
  local copies, waits for them, and re-layouts  8.4 us (7%)
  other arithmetic  2.5 us (2%)
  waiting for transfers between devices  1.98 us (2%)
    all_to_all x3, blocking collectives, exchange(): return lax.all_to_all(x, AXES, 0, 0, axis_index_groups=groups, tiled=True)  71 us
    ppermute x3, starting transfers between devices, on_device(): lax.ppermute(w, 'exp', swap)  10.7 us
    pallas_call x1, Pallas kernels, expert_partials(): pl.pallas_call(functools.partial(expert_kernel, float(width * n_ctx)), ou...  9.13 us
    all_to_all x1, starting transfers between devices, exchange(): return lax.all_to_all(x, AXES, 0, 0, axis_index_groups=groups, tiled=True)  4.41 us
    all_to_all x1, starting transfers between devices, on_device(): parts = lax.all_to_all(parts, 'ctx', 0, 0, tiled=True)  4.26 us
    pallas_call x1, Pallas kernels, attention_parts(): pl.pallas_call(functools.partial(attention_kernel, n_ctx), out_shape=jax....  3.92 us
  transfers between devices with their start and end apart: 5, of which 1 were waited for; matrix products, arithmetic and copies ran while one was open for 5% of the time, Pallas kernels for 0%

profile of v1, /device:TPU:75, one launch (start us, length us, event | category | flops | bytes accessed | tf_op | source)
XLA Modules:
  0.0 118.2 jit_solution(2967383509709830470)
XLA Ops:
  0.0 3.9 %attention_parts.1 = f32[8,16,128]{2,1,0:T(8,128)} custom-call(s32[2,2]{1,0:T(2,128)} %table.1, s32[2]{0:T(128)} %lengths.1, s32[1]{0:T(128)} %bitcast.place, bf16[2,6144]{1,0:T(2,128)(2,1)} %q_ref.1, bf16[1,3,64,1024]{3,2,1,0:T(8,128)(2,1)} %k_ref.1, bf16[1,3,64,1024]{3,2,1,0:T(8,128)(2,1)} %v_ref.1), custom_call_target="tpu_custom_call" | custom-call | tf_op jit(solution)/shard_map/attention_parts/pallas_call | solution.py:110
  3.9 4.3 %all-to-all-start = ((f32[4,2,16,128]{3,2,1,0:T(8,128)}), f32[4,2,16,128]{3,2,1,0:T(8,128)S(1)}, u32[]{:S(2)}, u32[]{:S(2)}) async-start(f32[4,2,16,128]{3,2,1,0:T(8,128)} %bitcast.24), calls=%async_computation | async-start | bytes 131072 | tf_op jit(solution)/shard_map/all_to_all | solution.py:341
  8.2 1.3 %reshape.41.gain_ref = bf16[1,6144]{1,0:T(2,128)(2,1)} reshape(bf16[6144]{0:T(1024)(128)(2,1)} %param.19) | data formatting | bytes 24576 | tf_op jit(solution)/shard_map/reshape | solution.py:343
  9.5 2.0 %all-to-all-done.parts_ref = f32[4,2,16,128]{3,2,1,0:T(8,128)S(1)} async-done(((f32[4,2,16,128]{3,2,1,0:T(8,128)}), f32[4,2,16,128]{3,2,1,0:T(8,128)S(1)}, u32[]{:S(2)}, u32[]{:S(2)}) %all-to-all-start) | async-done | bytes 65568 | tf_op jit(solution)/shard_map/all_to_all | solution.py:341
  11.5 0.0 copy-start.2
  11.5 0.6 copy-done.2
  12.1 1.7 %merge_parts.1 = (bf16[2,1664]{1,0:T(2,128)(2,1)}, bf16[2,1536]{1,0:T(2,128)(2,1)}) custom-call(s32[1]{0:T(128)} %bitcast.place, f32[4,2,16,128]{3,2,1,0:T(8,128)} %copy-done.2, bf16[2,6144]{1,0:T(2,128)(2,1)} %residual_ref.1, bf16[1,6144]{1,0:T(2,128)(2,1)} %reshape.41.gain_ref), custom_call_target="tpu_custom_call" | custom-call | tf_op jit(solution)/shard_map/merge_parts/pallas_call | solution.py:163
  13.8 0.8 broadcast_in_dim.32
  14.6 28.4 %all_to_all.25 = bf16[32,2,1664]{2,1,0:T(2,128)(2,1)S(1)} all-to-all(bf16[32,2,1664]{2,1,0:T(2,128)(2,1)S(1)} %broadcast_in_dim.32), channel_id=1, replica_groups={{0,4,8,12,128,132,136,140,256,260,264,268,384,388,392,396,32,36,40,44,1..., dimensions={0} | all-to-all | bytes 425984 | tf_op jit(solution)/shard_map/all_to_all | solution.py:347
  43.0 0.1 reshape.42
  43.1 1.4 %broadcast_in_dim.33 = bf16[8,2,32,1664]{3,2,1,0:T(8,128)(2,1)} broadcast(bf16[2,32,1664]{2,1,0:T(8,128)(2,1)S(1)} %reshape.42), dimensions={1,2,3} | broadcast | bytes 1916928 | tf_op jit(solution)/shard_map/broadcast_in_dim | solution.py:351
  44.5 0.0 copy-start.1
  44.5 0.0 copy-start.3
  44.5 0.0 copy-start.4
  44.5 0.0 copy-start.6
  44.5 4.4 %all-to-all-start.2 = ((bf16[8,2,32,1664]{3,2,1,0:T(8,128)(2,1)}), bf16[8,2,32,1664]{3,2,1,0:T(8,128)(2,1)S(1)}, u32[]{:S(2)}, u32[]{:S(2)}) async-start(bf16[8,2,32,1664]{3,2,1,0:T(8,128)(2,1)} %broadcast_in_dim.33), calls=%async_computation.2 | async-start | bytes 3407872 | tf_op jit(solution)/shard_map/all_to_all | solution.py:347
  48.9 0.0 copy-done.1
  48.9 6.4 %collective-permute-start = (bf16[1,96,6144]{2,1,0:T(8,128)(2,1)S(1)}, bf16[1,96,6144]{2,1,0:T(8,128)(2,1)}, u32[]{:S(2)}, u32[]{:S(2)}) collective-permute-start(bf16[1,96,6144]{2,1,0:T(8,128)(2,1)S(1)} %copy-done.1), channel_id=1, source_target_pairs={{0,1},{1,0},{2,3},{3,2},{4,5},{5,4},{6,7},{7,6},{8,9},{9,8},{10,11... | collective-permute-start | bytes 3538952 | tf_op jit(solution)/shard_map/ppermute | solution.py:333
  55.3 1.9 %collective-permute-start.1 = (bf16[1,96,6144]{2,1,0:T(8,128)(2,1)}, bf16[1,96,6144]{2,1,0:T(8,128)(2,1)}, u32[]{:S(2)}, u32[]{:S(2)}) collective-permute-start(bf16[1,96,6144]{2,1,0:T(8,128)(2,1)} %up_a.1), channel_id=1, source_target_pairs={{0,1},{1,0},{2,3},{3,2},{4,5},{5,4},{6,7},{7,6},{8,9},{9,8},{10,11... | collective-permute-start | bytes 3538952 | tf_op jit(solution)/shard_map/ppermute | solution.py:333
  57.2 2.4 %collective-permute-start.2 = (bf16[1,96,6144]{2,1,0:T(8,128)(2,1)}, bf16[1,96,6144]{2,1,0:T(8,128)(2,1)}, u32[]{:S(2)}, u32[]{:S(2)}) collective-permute-start(bf16[1,96,6144]{2,1,0:T(8,128)(2,1)} %down_a.1), channel_id=1, source_target_pairs={{0,1},{1,0},{2,3},{3,2},{4,5},{5,4},{6,7},{7,6},{8,9},{9,8},{10,11... | collective-permute-start | bytes 3538952 | tf_op jit(solution)/shard_map/ppermute | solution.py:333
  59.7 0.0 copy-done.3
  59.7 0.0 copy-done.4
  59.7 0.0 copy-done.6
  59.7 0.7 fusion.2
  60.4 1.4 %pad_add_fusion = s32[2]{0:T(128)S(1)} fusion(s32[1]{0:T(128)} %get-tuple-element.10, s32[1]{0:T(128)} %get-tuple-element.9), kind=kLoop, calls=%fused_computation.10 | loop fusion | flops 2 | bytes 16 | tf_op jit(solution)/shard_map/stack | solution.py:296
  61.8 0.1 select_reduce_fusion
  61.9 0.1 reshape.46
  62.0 0.1 copy.56
  62.1 0.1 slice.28
  62.2 0.1 fusion.1
  62.3 0.1 fusion
  62.4 0.1 copy.58
  62.5 0.1 concatenate.12
  62.6 0.5 copy.59
  63.1 1.1 copy.60
  64.3 0.0 collective-permute-done.gate_b
  64.3 0.0 collective-permute-done.1.up_b
  64.3 0.0 collective-permute-done.2.down_b
  64.3 0.0 all-to-all-done.2
  64.3 0.0 copy-start
  64.3 1.2 %copy-done = bf16[8,2,32,1664]{3,2,1,0:T(8,128)(2,1)} copy-done((bf16[8,2,32,1664]{3,2,1,0:T(8,128)(2,1)}, bf16[8,2,32,1664]{3,2,1,0:T(8,128)(2,1)S(1)}, u32[]{:S(2)}) %copy-start) | copy-done | bytes 1703960
  65.5 9.1 %expert_partials.1 = bf16[2,4,2,32,1536]{4,3,2,1,0:T(8,128)(2,1)} custom-call(s32[1]{0:T(128)} %bitcast.2.core, bf16[2,4,2,32,1664]{4,3,2,1,0:T(8,128)(2,1)} %bitcast.21, f32[128,2]{1,0:T(8,128)} %bitcast.23, bf16[1,96,6144]{2,1,0:T(8,128)(2,1)} %gate_a.1, bf16[1,96,6144]{2,1,0:T(8,128)(2,1)} %collective-permute-done.gate_b, bf16[1,96,6144]{2,1,0:T(8,128)(2,1)} %up_a.1, ...), custom_call_target="tpu_custom_call" | custom-call | flops 905969664 | bytes 7077888 | tf_op jit(solution)/shard_map/expert_partials/pallas_call | solution.py:259
  74.7 16.3 %all_to_all.26 = bf16[8,2,32,1536]{3,2,1,0:T(8,128)(2,1)S(1)} all-to-all(bf16[8,2,32,1536]{3,2,1,0:T(8,128)(2,1)} %bitcast.22), channel_id=1, replica_groups={{0,2,64,66,16,18,80,82},{4,6,68,70,20,22,84,86},{8,10,72,74,24,26,88,90..., dimensions={0} | all-to-all | bytes 3145728 | tf_op jit(solution)/shard_map/all_to_all | solution.py:347
  91.0 0.2 reduce_sum.31
  91.2 0.1 reshape.49
  91.3 26.3 %all_to_all.27 = bf16[32,2,1536]{2,1,0:T(2,128)(2,1)S(1)} all-to-all(bf16[32,2,1536]{2,1,0:T(2,128)(2,1)S(1)} %reshape.49), channel_id=1, replica_groups={{0,4,8,12,128,132,136,140,256,260,264,268,384,388,392,396,32,36,40,44,1..., dimensions={0} | all-to-all | bytes 393216 | tf_op jit(solution)/shard_map/all_to_all | solution.py:347
  117.6 0.0 copy-done.5
  117.6 0.6 add_convert_fusion
  (9 shorter events, 0.1 us)
Async XLA Ops:
  3.9 7.6 %all-to-all-start = ((f32[4,2,16,128]{3,2,1,0:T(8,128)}), f32[4,2,16,128]{3,2,1,0:T(8,128)S(1)}, u32[]{:S(2)}, u32[]{:S(2)}) async-start(f32[4,2,16,128]{3,2,1,0:T(8,128)} %bitcast.24), calls=%async_computation | async-start | bytes 131072 | tf_op jit(solution)/shard_map/all_to_all | solution.py:341
  11.5 0.6 copy-start.2
  44.5 4.4 %copy-start.1 = (bf16[1,96,6144]{2,1,0:T(8,128)(2,1)S(1)}, bf16[1,96,6144]{2,1,0:T(8,128)(2,1)}, u32[]{:S(2)}) copy-start(bf16[1,96,6144]{2,1,0:T(8,128)(2,1)} %gate_a.1) | copy-start | bytes 3538948
  44.5 15.2 %copy-start.3 = (s32[16,16,4]{1,2,0:T(4,128)S(1)}, s32[16,16,4]{1,2,0:T(4,128)}, u32[]{:S(2)}) copy-start(s32[16,16,4]{1,2,0:T(4,128)} %param.23) | copy-start | bytes 12292
  44.5 15.2 %copy-start.4 = (f32[16,16,4]{1,2,0:T(4,128)S(1)}, f32[16,16,4]{1,2,0:T(4,128)}, u32[]{:S(2)}) copy-start(f32[16,16,4]{1,2,0:T(4,128)} %param.24) | copy-start | bytes 12292
  44.5 15.3 %copy-start.6 = (s32[16]{0:T(128)S(1)}, s32[16]{0:T(128)}, u32[]{:S(2)}) copy-start(s32[16]{0:T(128)} %param.25) | copy-start | bytes 196
  44.5 19.8 %all-to-all-start.2 = ((bf16[8,2,32,1664]{3,2,1,0:T(8,128)(2,1)}), bf16[8,2,32,1664]{3,2,1,0:T(8,128)(2,1)S(1)}, u32[]{:S(2)}, u32[]{:S(2)}) async-start(bf16[8,2,32,1664]{3,2,1,0:T(8,128)(2,1)} %broadcast_in_dim.33), calls=%async_computation.2 | async-start | bytes 3407872 | tf_op jit(solution)/shard_map/all_to_all | solution.py:347
  48.9 15.4 %collective-permute-start = (bf16[1,96,6144]{2,1,0:T(8,128)(2,1)S(1)}, bf16[1,96,6144]{2,1,0:T(8,128)(2,1)}, u32[]{:S(2)}, u32[]{:S(2)}) collective-permute-start(bf16[1,96,6144]{2,1,0:T(8,128)(2,1)S(1)} %copy-done.1), channel_id=1, source_target_pairs={{0,1},{1,0},{2,3},{3,2},{4,5},{5,4},{6,7},{7,6},{8,9},{9,8},{10,11... | collective-permute-start | bytes 3538952 | tf_op jit(solution)/shard_map/ppermute | solution.py:333
  55.3 9.0 %collective-permute-start.1 = (bf16[1,96,6144]{2,1,0:T(8,128)(2,1)}, bf16[1,96,6144]{2,1,0:T(8,128)(2,1)}, u32[]{:S(2)}, u32[]{:S(2)}) collective-permute-start(bf16[1,96,6144]{2,1,0:T(8,128)(2,1)} %up_a.1), channel_id=1, source_target_pairs={{0,1},{1,0},{2,3},{3,2},{4,5},{5,4},{6,7},{7,6},{8,9},{9,8},{10,11... | collective-permute-start | bytes 3538952 | tf_op jit(solution)/shard_map/ppermute | solution.py:333
  57.2 7.1 %collective-permute-start.2 = (bf16[1,96,6144]{2,1,0:T(8,128)(2,1)}, bf16[1,96,6144]{2,1,0:T(8,128)(2,1)}, u32[]{:S(2)}, u32[]{:S(2)}) collective-permute-start(bf16[1,96,6144]{2,1,0:T(8,128)(2,1)} %down_a.1), channel_id=1, source_target_pairs={{0,1},{1,0},{2,3},{3,2},{4,5},{5,4},{6,7},{7,6},{8,9},{9,8},{10,11... | collective-permute-start | bytes 3538952 | tf_op jit(solution)/shard_map/ppermute | solution.py:333
  64.3 1.2 %copy-start = (bf16[8,2,32,1664]{3,2,1,0:T(8,128)(2,1)}, bf16[8,2,32,1664]{3,2,1,0:T(8,128)(2,1)S(1)}, u32[]{:S(2)}) copy-start(bf16[8,2,32,1664]{3,2,1,0:T(8,128)(2,1)S(1)} %all-to-all-done.2) | copy-start | bytes 5111812
  91.0 26.6 %copy-start.5 = (bf16[2,1536]{1,0:T(2,128)(2,1)S(1)}, bf16[2,1536]{1,0:T(2,128)(2,1)}, u32[]{:S(2)}) copy-start(bf16[2,1536]{1,0:T(2,128)(2,1)} %get-tuple-element.7) | copy-start | bytes 18436

commit v2 on v1

v2 whole, which is shorter than its diff:
```python
import functools

import jax
import jax.numpy as jnp
import numpy as np
from jax import lax
from jax.experimental import pallas as pl
from jax.experimental.pallas import tpu as pltpu
from jax.sharding import PartitionSpec as P

HEADS = 48
KV_HEADS = 8
HEAD_DIM = 128
GROUP = HEADS // KV_HEADS
EPSILON = 1e-05
NEGATIVE = -1e30
ROWS = 16
LANES = 128
KERNEL_VMEM = 16 << 20
AXES = ("req", "ctx", "exp")
F32 = jnp.float32
BF16 = jnp.bfloat16


def in_vmem(x):
    return pltpu.with_memory_space_constraint(x, pltpu.VMEM)


def in_hbm(x):
    return pltpu.with_memory_space_constraint(x, pltpu.HBM)


def exchange_groups(n_req, n_ctx, n_exp):
    cols = n_exp // 2

    def device(z, x, y, core):
        z, x, y = (z + core) % n_req, (x + core) % n_ctx, (y + core) % cols
        return (z * n_ctx + x) * n_exp + y * 2 + core

    near = [
        [
            device(2 * zh + zl, 2 * xh + xl, 2 * yh + yl, core)
            for xl in (0, 1)
            for zl in (0, 1)
            for yl in (0, 1)
        ]
        for core in (0, 1)
        for xh in range(n_ctx // 2)
        for zh in range(n_req // 2)
        for yh in range(cols // 2)
    ]
    far = [
        [
            device(2 * zh + zl, 2 * xh + xl, 2 * yh + yl, core)
            for xh in range(n_ctx // 2)
            for zh in range(n_req // 2)
            for yh in range(cols // 2)
        ]
        for core in (0, 1)
        for xl in (0, 1)
        for zl in (0, 1)
        for yl in (0, 1)
    ]
    return near, far


def attention_kernel(
    n_ctx, table, lengths, place, q_ref, k_ref, v_ref, residual_ref, out_ref, own_ref, heads
):
    width = own_ref.shape[1]
    own_ref[...] = residual_ref[:, pl.ds(pl.multiple_of(place[0] * width, width), width)]
    requests, slots, page_rows = q_ref.shape[0], k_ref.shape[1], k_ref.shape[2]
    span = table.shape[1]
    positions = slots * page_rows
    heads[...] = jnp.zeros_like(heads)
    queries = q_ref[...].astype(F32)
    for r in range(requests):
        for h in range(HEADS):
            row = (h // GROUP) * ROWS + r * GROUP + h % GROUP
            heads[row : row + 1, :] = queries[r : r + 1, h * HEAD_DIM : (h + 1) * HEAD_DIM]
    at = lax.broadcasted_iota(jnp.int32, (ROWS, positions), 1)
    row_id = lax.broadcasted_iota(jnp.int32, (ROWS, positions), 0)
    slot, offset = at // page_rows, at % page_rows
    live = None
    for r in range(requests):
        seen = None
        for s in range(span):
            position = (s * n_ctx + place[0]) * page_rows + offset
            here = (slot == table[r, s]) & (position < lengths[r])
            seen = here if seen is None else seen | here
        live = seen if live is None else jnp.where(row_id < r * GROUP, live.astype(jnp.int32), seen.astype(jnp.int32)) > 0
    out_row = lax.broadcasted_iota(jnp.int32, (ROWS, LANES), 0)
    diagonal = out_row == lax.broadcasted_iota(jnp.int32, (ROWS, LANES), 1)
    live = jnp.concatenate([live] * KV_HEADS, axis=0)
    keys = k_ref[0].reshape(positions, KV_HEADS * HEAD_DIM)
    values = v_ref[0].reshape(positions, KV_HEADS * HEAD_DIM)
    query = heads[...].astype(BF16)

    def rows(k):
        return slice(k * ROWS, (k + 1) * ROWS)

    def lanes(k):
        return slice(k * HEAD_DIM, (k + 1) * HEAD_DIM)

    scores = jnp.concatenate(
        [
            lax.dot_general(
                query[rows(k)],
                keys[:, lanes(k)],
                (((1,), (1,)), ((), ())),
                preferred_element_type=F32,
            )
            for k in range(KV_HEADS)
        ],
        axis=0,
    )
    scores = jnp.where(live, scores * HEAD_DIM ** (-0.5), NEGATIVE)
    top = jnp.max(scores, axis=1, keepdims=True)
    weights = jnp.where(live, jnp.exp(scores - top), 0.0)
    total = jnp.sum(weights, axis=1, keepdims=True)
    high = weights.astype(BF16)
    low = (weights - high.astype(F32)).astype(BF16)
    used = requests * GROUP
    for k in range(KV_HEADS):
        mixes = jnp.dot(
            jnp.concatenate([high[rows(k)], low[rows(k)]], axis=0),
            values[:, lanes(k)],
            preferred_element_type=F32,
        )
        mixes = mixes[:ROWS] + mixes[ROWS:]
        top_row = jnp.sum(jnp.where(diagonal, top[rows(k)], 0.0), axis=0, keepdims=True)
        total_row = jnp.sum(jnp.where(diagonal, total[rows(k)], 0.0), axis=0, keepdims=True)
        out_ref[k] = jnp.where(
            out_row < used, mixes, jnp.where(out_row == used, top_row, total_row)
        )


def attention_parts(
    queries, key_pages, value_pages, block_table, lengths, residual, place, n_ctx
):
    smem = pl.BlockSpec(memory_space=pltpu.SMEM)
    vmem = pl.BlockSpec(memory_space=pltpu.VMEM)
    return pl.pallas_call(
        functools.partial(attention_kernel, n_ctx),
        out_shape=(
            pltpu.VMEM((KV_HEADS, ROWS, HEAD_DIM), F32),
            pltpu.VMEM((residual.shape[0], residual.shape[1] // n_ctx), BF16),
        ),
        in_specs=[smem, smem, smem, vmem, vmem, vmem, vmem],
        out_specs=(vmem, vmem),
        scratch_shapes=[pltpu.VMEM((KV_HEADS * ROWS, HEAD_DIM), F32)],
        compiler_params=pltpu.CompilerParams(vmem_limit_bytes=KERNEL_VMEM),
        name="attention_parts",
    )(
        in_hbm(block_table),
        in_hbm(lengths),
        place,
        *(in_hbm(x) for x in (queries, key_pages, value_pages, residual)),
    )


def merge_kernel(place, parts_ref, residual_ref, gain_ref, piece_ref, stream_ref, merged):
    n_src, kv_here = parts_ref.shape[0], parts_ref.shape[1]
    requests, width = stream_ref.shape
    used = requests * GROUP
    diagonal = lax.broadcasted_iota(jnp.int32, (ROWS, LANES), 0) == lax.broadcasted_iota(
        jnp.int32, (ROWS, LANES), 1
    )

    def column(row):
        return jnp.sum(jnp.where(diagonal, row, 0.0), axis=1, keepdims=True)

    for k in range(kv_here):
        tops = [column(parts_ref[s, k, used : used + 1, :]) for s in range(n_src)]
        totals = [column(parts_ref[s, k, used + 1 : used + 2, :]) for s in range(n_src)]
        top = functools.reduce(jnp.maximum, tops)
        scales = [jnp.exp(t - top) for t in tops]
        mixes = sum(parts_ref[s, k] * scales[s] for s in range(n_src))
        total = sum(totals[s] * scales[s] for s in range(n_src))
        mixes = mixes / total
        for r in range(requests):
            for g in range(GROUP):
                at = (k * GROUP + g) * HEAD_DIM
                merged[r : r + 1, at : at + HEAD_DIM] = mixes[r * GROUP + g : r * GROUP + g + 1, :]
    columns = pl.ds(pl.multiple_of(place[0] * width, width), width)
    stream = (residual_ref[...].astype(F32) + merged[...]).astype(BF16)
    stream_ref[...] = stream
    wide = stream.astype(F32)
    scaled = (wide * gain_ref[:, columns].astype(F32)).astype(BF16)
    square = jnp.sum(wide * wide, axis=1, keepdims=True)
    first = square.astype(BF16).astype(F32)
    second = (square - first).astype(BF16).astype(F32)
    third = square - first - second
    lane = lax.broadcasted_iota(jnp.int32, (requests, LANES), 1)
    spread = jnp.where(
        lane == 0, first, jnp.where(lane == 1, second, jnp.where(lane == 2, third, 0.0))
    )
    spread = spread.astype(BF16)
    for copy in range(piece_ref.shape[0]):
        piece_ref[copy, :, :width] = scaled
        piece_ref[copy, :, width:] = spread


def merge_parts(parts, residual, gain, place, width, copies):
    requests = residual.shape[0]
    smem = pl.BlockSpec(memory_space=pltpu.SMEM)
    vmem = pl.BlockSpec(memory_space=pltpu.VMEM)
    return pl.pallas_call(
        merge_kernel,
        out_shape=(
            pltpu.VMEM((copies, requests, width + LANES), BF16),
            jax.ShapeDtypeStruct((requests, width), BF16),
        ),
        in_specs=[smem, vmem, vmem, vmem],
        out_specs=(vmem, vmem),
        scratch_shapes=[pltpu.VMEM((requests, width), F32)],
        compiler_params=pltpu.CompilerParams(vmem_limit_bytes=KERNEL_VMEM),
        name="merge_parts",
    )(place, in_vmem(parts), in_vmem(residual), gain)


def row_shares(table, blocks, core, n_req, rows):
    top, entries = table.shape[0] // 2, table.shape[1]
    per_exp = entries // (n_req * 2)
    requests = entries // per_exp // n_req
    half_z, half_y = n_req // 2, per_exp // 4
    row = lax.broadcasted_iota(jnp.int32, (entries, rows), 1)
    entry = lax.broadcasted_iota(jnp.int32, (entries, rows), 0)
    request, row = row % requests, row // requests
    yh, row = row % half_y, row // half_y
    zh, row = row % half_z, row // half_z
    yl, zl = row % 2, row // 2
    z = (2 * zh + zl + core) % n_req
    y = (2 * yh + yl + core) % (per_exp // 2)
    wanted = ((2 * y + core) * n_req + z) * requests + request
    pick = jnp.where(entry == wanted, 1.0, 0.0).astype(BF16)
    lines = []
    for block in blocks:
        named = table[:top] == block.astype(F32)
        line = jnp.sum(jnp.where(named, table[top:], 0.0), axis=0, keepdims=True)
        first = line.astype(BF16)
        second = (line - first.astype(F32)).astype(BF16)
        third = (line - first.astype(F32) - second.astype(F32)).astype(BF16)
        lines += [first, second, third]
    lines.append(jnp.zeros((16 - len(lines), entries), BF16))
    picked = jnp.dot(jnp.concatenate(lines, axis=0), pick, preferred_element_type=F32)
    return [picked[i : i + 1] + picked[i + 1 : i + 2] + picked[i + 2 : i + 3] for i in (0, 3)]


def expert_kernel(model_width, n_req, exp_index, block_expert, tokens_ref, table_ref, *refs):
    sources, out_ref, held, arrived = refs[:6], refs[6], refs[7:13], refs[13]
    copies = [
        pltpu.make_async_copy(source, here, arrived.at[i])
        for i, (source, here) in enumerate(zip(sources, held))
    ]
    for copy in copies:
        copy.start()
    n_xl, quarters, n_xh, far_rows, width = out_ref.shape
    n_ctx, rows, hidden = n_xl * n_xh, quarters * far_rows, held[0].shape[1]
    contract = (((1,), (1,)), ((), ()))
    ones = jnp.ones((8, LANES), BF16)

    own = exp_index[0]
    core = lax.rem(own, 2)
    blocks = (block_expert[own], block_expert[own + 1 - 2 * core])
    shares = row_shares(table_ref[...], blocks, core, n_req, rows)

    def at(chunk):
        column = lax.rem(chunk + n_ctx - core, n_ctx)
        return column % n_xl, column // n_xl

    def added(total, term):
        return term if total is None else total + term

    squares = None
    for chunk in range(n_ctx):
        xl, xh = at(chunk)
        tokens = tokens_ref[xl, :, xh, :, width:].reshape(rows, LANES)
        squares = added(
            squares, lax.dot_general(ones, tokens, contract, preferred_element_type=F32)
        )
    scale = lax.rsqrt(squares[:1] / model_width + EPSILON)
    active = []
    for b in range(2):
        for copy in copies[2 * b : 2 * b + 2]:
            copy.wait()
        products = None
        for chunk in range(n_ctx):
            xl, xh = at(chunk)
            tokens = tokens_ref[xl, :, xh, :, :width].reshape(rows, width)
            columns = slice(chunk * width, (chunk + 1) * width)
            wide = jnp.concatenate([w[0, :, columns] for w in held[2 * b : 2 * b + 2]], axis=0)
            products = added(
                products,
                lax.dot_general(wide, tokens, contract, preferred_element_type=F32),
            )
        gate, up = products[:hidden] * scale, products[hidden:] * scale
        active.append(gate / (1.0 + jnp.exp(-gate)) * up * shares[b])
    active.append(jnp.zeros((-2 * hidden % LANES, rows), F32))
    active = jnp.concatenate(active, axis=0).T[:, : 2 * hidden].astype(BF16)
    for copy in copies[4:]:
        copy.wait()
    for chunk in range(n_ctx):
        xl, xh = at(chunk)
        columns = slice(chunk * width, (chunk + 1) * width)
        down = jnp.concatenate([w[0, :, columns] for w in held[4:]], axis=0)
        total = jnp.dot(active, down, preferred_element_type=F32).astype(BF16)
        out_ref[xl, :, xh] = total.reshape(quarters, far_rows, width)


def routing_table(expert_routes, route_weights):
    top = expert_routes.shape[2]
    table = jnp.concatenate([expert_routes.astype(F32), route_weights], axis=2)
    return table.transpose(2, 0, 1).reshape(2 * top, -1)


def expert_partials(tokens, table, block_expert, weights, exp_index, n_req):
    n_xl, quarters, n_xh, far_rows, padded = tokens.shape
    width = padded - LANES
    rows, model_width = quarters * far_rows, width * n_xl * n_xh
    hidden = weights[0].shape[1]
    smem = pl.BlockSpec(memory_space=pltpu.SMEM)
    vmem = pl.BlockSpec(memory_space=pltpu.VMEM)
    return pl.pallas_call(
        functools.partial(expert_kernel, float(model_width), n_req),
        out_shape=pltpu.VMEM((n_xl, quarters, n_xh, far_rows, width), BF16),
        in_specs=[smem, smem, vmem, vmem]
        + [pl.BlockSpec(memory_space=pltpu.HBM)] * len(weights),
        out_specs=vmem,
        scratch_shapes=[pltpu.VMEM(w.shape, w.dtype) for w in weights]
        + [pltpu.SemaphoreType.DMA((len(weights),))],
        compiler_params=pltpu.CompilerParams(vmem_limit_bytes=KERNEL_VMEM),
        cost_estimate=pl.CostEstimate(
            flops=12 * rows * hidden * model_width,
            bytes_accessed=12 * hidden * model_width,
            transcendentals=0,
        ),
        name="expert_partials",
    )(
        exp_index, block_expert, in_vmem(tokens), in_vmem(table), *(in_hbm(w) for w in weights)
    )


def on_device(
    groups,
    queries,
    key_pages,
    value_pages,
    block_table,
    context_lengths,
    residual,
    norm_gain,
    gate_blocks,
    up_blocks,
    down_blocks,
    expert_routes,
    route_weights,
    block_expert,
):
    near, far = groups
    n_req, n_ctx, n_exp = (lax.axis_size(a) for a in AXES)
    requests, model_width = queries.shape
    width = model_width // n_ctx
    place = lax.axis_index("ctx")
    exp_index = lax.axis_index("exp")
    n_near, n_far = len(near[0]), len(far[0])
    far_rows = n_far // 2 * requests

    swap = [(i, i ^ 1) for i in range(n_exp)]
    gate_other, up_other, down_other = (
        lax.ppermute(w, "exp", swap) for w in (gate_blocks, up_blocks, down_blocks)
    )

    parts, residual = attention_parts(
        queries,
        key_pages,
        value_pages,
        block_table,
        context_lengths,
        residual,
        place[None],
        n_ctx,
    )
    parts = parts.reshape(n_ctx, KV_HEADS // n_ctx, ROWS, HEAD_DIM)
    parts = lax.all_to_all(parts, "ctx", 0, 0, tiled=True)
    piece, stream = merge_parts(
        parts, residual, norm_gain.reshape(1, model_width), place[None], width, n_far
    )

    def exchange(x, groups):
        return lax.all_to_all(x, AXES, 0, 0, axis_index_groups=groups, tiled=True)

    tokens = exchange(piece, far)
    tokens = tokens.reshape(2, far_rows, width + LANES)
    tokens = exchange(jnp.broadcast_to(tokens, (n_near,) + tokens.shape), near)
    tokens = tokens.reshape(2, n_near // 2, 2, far_rows, width + LANES)
    partials = expert_partials(
        tokens,
        routing_table(expert_routes, route_weights),
        block_expert,
        (gate_blocks, up_blocks, gate_other, up_other, down_blocks, down_other),
        exp_index[None],
        n_req,
    )
    partials = exchange(partials.reshape(n_near, 2, far_rows, width), near)
    partials = jnp.sum(partials.astype(F32), axis=0).astype(BF16)
    partials = exchange(partials.reshape(n_far, requests, width), far)
    expert_sum = jnp.sum(partials.astype(F32), axis=0)
    return (stream.astype(F32) + expert_sum).astype(BF16)


def solution(mesh):
    in_specs = (
        P(("req", "exp"), None),
        P(("req", "exp"), "ctx", None, None),
        P(("req", "exp"), "ctx", None, None),
        P(("req", "exp"), "ctx"),
        P(("req", "exp")),
        P(("req", "exp"), None),
        P(),
        P("exp", ("req", "ctx"), None),
        P("exp", ("req", "ctx"), None),
        P("exp", ("req", "ctx"), None),
        P(),
        P(),
        P(),
    )
    out_specs = P(("req", "exp"), "ctx")
    groups = exchange_groups(*(mesh.shape[a] for a in AXES))
    return jax.shard_map(
        functools.partial(on_device, groups),
        mesh=mesh,
        in_specs=in_specs,
        out_specs=out_specs,
        check_vma=False,
    )
```

time: 119 us -> 109 us (0.916)
  the two profiles are of different devices: /device:TPU:75 before, /device:TPU:3 now
where the time goes in v2:
time: 109 us; the launch traced here: 108 us
  blocking collectives  71.9 us (66%)
  starting transfers between devices  17 us (16%)
  Pallas kernels  8.24 us (8%)
  waiting for transfers between devices  7.58 us (7%)
  local copies, waits for them, and re-layouts  2.37 us (2%)
    all_to_all x3, blocking collectives, exchange(): return lax.all_to_all(x, AXES, 0, 0, axis_index_groups=groups, tiled=True)  71.9 us
    all_to_all x1, starting transfers between devices, exchange(): return lax.all_to_all(x, AXES, 0, 0, axis_index_groups=groups, tiled=True)  6.54 us
    ppermute x3, starting transfers between devices, on_device(): lax.ppermute(w, 'exp', swap)  6.24 us
    pallas_call x1, Pallas kernels, expert_partials(): pl.pallas_call(functools.partial(expert_kernel, float(model_width), n_req...  5.71 us
    all_to_all x1, starting transfers between devices, on_device(): parts = lax.all_to_all(parts, 'ctx', 0, 0, tiled=True)  4.26 us
    ppermute x3, waiting for transfers between devices, on_device(): lax.ppermute(w, 'exp', swap)  2.97 us
    all_to_all x1, waiting for transfers between devices, on_device(): parts = lax.all_to_all(parts, 'ctx', 0, 0, tiled=True)  2.57 us
    pallas_call x1, Pallas kernels, attention_parts(): pl.pallas_call(functools.partial(attention_kernel, n_ctx), out_shape=(plt...  2.3 us
  transfers between devices with their start and end apart: 5, of which 4 were waited for; matrix products, arithmetic and copies ran while one was open for 1% of the time, Pallas kernels for 0%

profile of v2, /device:TPU:3, one launch (start us, length us, event | category | flops | bytes accessed | tf_op | source)
XLA Modules:
  0.0 108.1 jit_solution(17152844612557785373)
XLA Ops:
  0.0 2.3 %attention_parts.1 = (f32[8,16,128]{2,1,0:T(8,128)}, bf16[2,1536]{1,0:T(2,128)(2,1)S(1)}) custom-call(s32[2,2]{1,0:T(2,128)} %table.1, s32[2]{0:T(128)} %lengths.1, s32[1]{0:T(128)} %bitcast.place, bf16[2,6144]{1,0:T(2,128)(2,1)} %q_ref.1, bf16[1,3,64,1024]{3,2,1,0:T(8,128)(2,1)} %k_ref.1, bf16[1,3,64,1024]{3,2,1,0:T(8,128)(2,1)} %v_ref.1, ...), custom_call_target="tpu_custom_call" | custom-call | tf_op jit(solution)/shard_map/attention_parts/pallas_call | solution.py:143
  2.3 4.3 %all-to-all-start = ((f32[4,2,16,128]{3,2,1,0:T(8,128)}), f32[4,2,16,128]{3,2,1,0:T(8,128)S(1)}, u32[]{:S(2)}, u32[]{:S(2)}) async-start(f32[4,2,16,128]{3,2,1,0:T(8,128)} %bitcast.1), calls=%async_computation | async-start | bytes 131072 | tf_op jit(solution)/shard_map/all_to_all | solution.py:385
  6.6 0.7 reshape.22.gain_ref
  7.3 2.6 %all-to-all-done.parts_ref = f32[4,2,16,128]{3,2,1,0:T(8,128)S(1)} async-done(((f32[4,2,16,128]{3,2,1,0:T(8,128)}), f32[4,2,16,128]{3,2,1,0:T(8,128)S(1)}, u32[]{:S(2)}, u32[]{:S(2)}) %all-to-all-start) | async-done | bytes 65568 | tf_op jit(solution)/shard_map/all_to_all | solution.py:385
  9.9 0.2 merge_parts.1
  10.1 32.0 %all_to_all.25 = bf16[32,2,1664]{2,1,0:T(2,128)(2,1)S(1)} all-to-all(bf16[32,2,1664]{2,1,0:T(2,128)(2,1)S(1)} %get-tuple-element.12), channel_id=1, replica_groups={{0,4,8,12,128,132,136,140,256,260,264,268,384,388,392,396,32,36,40,44,1..., dimensions={0} | all-to-all | bytes 425984 | tf_op jit(solution)/shard_map/all_to_all | solution.py:391
  42.1 0.1 reshape.23
  42.2 1.4 %broadcast_in_dim.12 = bf16[8,2,32,1664]{3,2,1,0:T(8,128)(2,1)} broadcast(bf16[2,32,1664]{2,1,0:T(8,128)(2,1)S(1)} %reshape.23), dimensions={1,2,3} | broadcast | bytes 1916928 | tf_op jit(solution)/shard_map/broadcast_in_dim | solution.py:395
  43.6 0.0 copy-start.1
  43.6 0.0 copy-start.2
  43.6 0.0 copy-start.3
  43.6 0.0 copy-start
  43.6 6.5 %all-to-all-start.2 = ((bf16[8,2,32,1664]{3,2,1,0:T(8,128)(2,1)}), bf16[8,2,32,1664]{3,2,1,0:T(8,128)(2,1)S(1)}, u32[]{:S(2)}, u32[]{:S(2)}) async-start(bf16[8,2,32,1664]{3,2,1,0:T(8,128)(2,1)} %broadcast_in_dim.12), calls=%async_computation.2 | async-start | bytes 3407872 | tf_op jit(solution)/shard_map/all_to_all | solution.py:391
  50.2 0.0 copy-done.1
  50.2 1.9 %collective-permute-start = (bf16[1,96,6144]{2,1,0:T(8,128)(2,1)S(1)}, bf16[1,96,6144]{2,1,0:T(8,128)(2,1)}, u32[]{:S(2)}, u32[]{:S(2)}) collective-permute-start(bf16[1,96,6144]{2,1,0:T(8,128)(2,1)S(1)} %copy-done.1), channel_id=1, source_target_pairs={{0,1},{1,0},{2,3},{3,2},{4,5},{5,4},{6,7},{7,6},{8,9},{9,8},{10,11... | collective-permute-start | bytes 3538952 | tf_op jit(solution)/shard_map/ppermute | solution.py:371
  52.1 2.4 %collective-permute-start.1 = (bf16[1,96,6144]{2,1,0:T(8,128)(2,1)}, bf16[1,96,6144]{2,1,0:T(8,128)(2,1)}, u32[]{:S(2)}, u32[]{:S(2)}) collective-permute-start(bf16[1,96,6144]{2,1,0:T(8,128)(2,1)} %refs_1_.1), channel_id=1, source_target_pairs={{0,1},{1,0},{2,3},{3,2},{4,5},{5,4},{6,7},{7,6},{8,9},{9,8},{10,11... | collective-permute-start | bytes 3538952 | tf_op jit(solution)/shard_map/ppermute | solution.py:371
  54.5 1.9 %collective-permute-start.2 = (bf16[1,96,6144]{2,1,0:T(8,128)(2,1)}, bf16[1,96,6144]{2,1,0:T(8,128)(2,1)}, u32[]{:S(2)}, u32[]{:S(2)}) collective-permute-start(bf16[1,96,6144]{2,1,0:T(8,128)(2,1)} %refs_4_.1), channel_id=1, source_target_pairs={{0,1},{1,0},{2,3},{3,2},{4,5},{5,4},{6,7},{7,6},{8,9},{9,8},{10,11... | collective-permute-start | bytes 3538952 | tf_op jit(solution)/shard_map/ppermute | solution.py:371
  56.4 0.0 copy-done.2
  56.5 0.0 copy-done.3
  56.5 0.1 reshape.25.table_ref
  56.6 0.0 collective-permute-done.refs_2_
  56.6 0.7 collective-permute-done.1.refs_3_
  57.3 2.3 %collective-permute-done.2.refs_5_ = bf16[1,96,6144]{2,1,0:T(8,128)(2,1)} collective-permute-done((bf16[1,96,6144]{2,1,0:T(8,128)(2,1)}, bf16[1,96,6144]{2,1,0:T(8,128)(2,1)}, u32[]{:S(2)}, u32[]{:S(2)}) %collective-permute-start.2) | collective-permute-done | bytes 1179680 | tf_op jit(solution)/shard_map/ppermute | solution.py:371
  59.6 2.0 %all-to-all-done.2 = bf16[8,2,32,1664]{3,2,1,0:T(8,128)(2,1)S(1)} async-done(((bf16[8,2,32,1664]{3,2,1,0:T(8,128)(2,1)}), bf16[8,2,32,1664]{3,2,1,0:T(8,128)(2,1)S(1)}, u32[]{:S(2)}, u32[]{:S(2)}) %all-to-all-start.2) | async-done | bytes 1703968 | tf_op jit(solution)/shard_map/all_to_all | solution.py:391
  61.6 0.0 copy-done
  61.6 5.7 %expert_partials.1 = bf16[2,4,2,32,1536]{4,3,2,1,0:T(8,128)(2,1)S(1)} custom-call(s32[1]{0:T(128)} %bitcast.2.exp_index, s32[16]{0:T(128)S(1)} %copy-done, bf16[2,4,2,32,1664]{4,3,2,1,0:T(8,128)(2,1)S(1)} %bitcast.7, f32[8,256]{1,0:T(8,128)S(1)} %reshape.25.table_ref, bf16[1,96,6144]{2,1,0:T(8,128)(2,1)} %refs_0_.1, bf16[1,96,6144]{2,1,0:T(8,128)(2,1)} %refs_1_.1, ...), custom_call_target="tpu_custom_call" | custom-call | flops 905969664 | bytes 7077888 | tf_op jit(solution)/shard_map/expert_partials/pallas_call | solution.py:324
  67.3 17.7 %all_to_all.26 = bf16[8,2,32,1536]{3,2,1,0:T(8,128)(2,1)S(1)} all-to-all(bf16[8,2,32,1536]{3,2,1,0:T(8,128)(2,1)S(1)} %bitcast.8), channel_id=1, replica_groups={{0,2,64,66,16,18,80,82},{4,6,68,70,20,22,84,86},{8,10,72,74,24,26,88,90..., dimensions={0} | all-to-all | bytes 3145728 | tf_op jit(solution)/shard_map/all_to_all | solution.py:391
  85.1 0.2 reduce_sum.21
  85.3 0.1 reshape.27
  85.4 22.1 %all_to_all.27 = bf16[32,2,1536]{2,1,0:T(2,128)(2,1)S(1)} all-to-all(bf16[32,2,1536]{2,1,0:T(2,128)(2,1)S(1)} %reshape.27), channel_id=1, replica_groups={{0,4,8,12,128,132,136,140,256,260,264,268,384,388,392,396,32,36,40,44,1..., dimensions={0} | all-to-all | bytes 393216 | tf_op jit(solution)/shard_map/all_to_all | solution.py:391
  107.5 0.6 add_convert_fusion
  (4 shorter events, 0.1 us)
Async XLA Ops:
  2.3 7.6 %all-to-all-start = ((f32[4,2,16,128]{3,2,1,0:T(8,128)}), f32[4,2,16,128]{3,2,1,0:T(8,128)S(1)}, u32[]{:S(2)}, u32[]{:S(2)}) async-start(f32[4,2,16,128]{3,2,1,0:T(8,128)} %bitcast.1), calls=%async_computation | async-start | bytes 131072 | tf_op jit(solution)/shard_map/all_to_all | solution.py:385
  43.6 6.6 %copy-start.1 = (bf16[1,96,6144]{2,1,0:T(8,128)(2,1)S(1)}, bf16[1,96,6144]{2,1,0:T(8,128)(2,1)}, u32[]{:S(2)}) copy-start(bf16[1,96,6144]{2,1,0:T(8,128)(2,1)} %refs_0_.1) | copy-start | bytes 3538948
  43.6 12.8 %copy-start.2 = (s32[16,16,4]{1,2,0:T(4,128)S(1)}, s32[16,16,4]{1,2,0:T(4,128)}, u32[]{:S(2)}) copy-start(s32[16,16,4]{1,2,0:T(4,128)} %param.23) | copy-start | bytes 12292
  43.6 12.8 %copy-start.3 = (f32[16,16,4]{1,2,0:T(4,128)S(1)}, f32[16,16,4]{1,2,0:T(4,128)}, u32[]{:S(2)}) copy-start(f32[16,16,4]{1,2,0:T(4,128)} %param.24) | copy-start | bytes 12292
  43.6 18.0 %copy-start = (s32[16]{0:T(128)S(1)}, s32[16]{0:T(128)}, u32[]{:S(2)}) copy-start(s32[16]{0:T(128)} %block_expert.1) | copy-start | bytes 196
  43.6 18.0 %all-to-all-start.2 = ((bf16[8,2,32,1664]{3,2,1,0:T(8,128)(2,1)}), bf16[8,2,32,1664]{3,2,1,0:T(8,128)(2,1)S(1)}, u32[]{:S(2)}, u32[]{:S(2)}) async-start(bf16[8,2,32,1664]{3,2,1,0:T(8,128)(2,1)} %broadcast_in_dim.12), calls=%async_computation.2 | async-start | bytes 3407872 | tf_op jit(solution)/shard_map/all_to_all | solution.py:391
  50.2 6.4 %collective-permute-start = (bf16[1,96,6144]{2,1,0:T(8,128)(2,1)S(1)}, bf16[1,96,6144]{2,1,0:T(8,128)(2,1)}, u32[]{:S(2)}, u32[]{:S(2)}) collective-permute-start(bf16[1,96,6144]{2,1,0:T(8,128)(2,1)S(1)} %copy-done.1), channel_id=1, source_target_pairs={{0,1},{1,0},{2,3},{3,2},{4,5},{5,4},{6,7},{7,6},{8,9},{9,8},{10,11... | collective-permute-start | bytes 3538952 | tf_op jit(solution)/shard_map/ppermute | solution.py:371
  52.1 5.2 %collective-permute-start.1 = (bf16[1,96,6144]{2,1,0:T(8,128)(2,1)}, bf16[1,96,6144]{2,1,0:T(8,128)(2,1)}, u32[]{:S(2)}, u32[]{:S(2)}) collective-permute-start(bf16[1,96,6144]{2,1,0:T(8,128)(2,1)} %refs_1_.1), channel_id=1, source_target_pairs={{0,1},{1,0},{2,3},{3,2},{4,5},{5,4},{6,7},{7,6},{8,9},{9,8},{10,11... | collective-permute-start | bytes 3538952 | tf_op jit(solution)/shard_map/ppermute | solution.py:371
  54.5 5.1 %collective-permute-start.2 = (bf16[1,96,6144]{2,1,0:T(8,128)(2,1)}, bf16[1,96,6144]{2,1,0:T(8,128)(2,1)}, u32[]{:S(2)}, u32[]{:S(2)}) collective-permute-start(bf16[1,96,6144]{2,1,0:T(8,128)(2,1)} %refs_4_.1), channel_id=1, source_target_pairs={{0,1},{1,0},{2,3},{3,2},{4,5},{5,4},{6,7},{7,6},{8,9},{9,8},{10,11... | collective-permute-start | bytes 3538952 | tf_op jit(solution)/shard_map/ppermute | solution.py:371

commit v3 on v2

--- a/solution.py
+++ b/solution.py
@@ -64,15 +64,33 @@
     return near, far
 
 
-def attention_kernel(
-    n_ctx, table, lengths, place, q_ref, k_ref, v_ref, residual_ref, out_ref, own_ref, heads
-):
-    width = own_ref.shape[1]
-    own_ref[...] = residual_ref[:, pl.ds(pl.multiple_of(place[0] * width, width), width)]
+def started(sources, targets, arrived):
+    copies = [
+        pltpu.make_async_copy(source, target, arrived.at[i])
+        for i, (source, target) in enumerate(zip(sources, targets))
+    ]
+    for copy in copies:
+        copy.start()
+    return copies
+
+
+def attention_kernel(n_ctx, *refs):
+    sources, (out_ref, own_ref), heads, targets, arrived = (
+        refs[:6],
+        refs[6:8],
+        refs[8],
+        refs[9:15],
+        refs[15],
+    )
+    table, lengths, q_ref, k_ref, v_ref, residual_ref = targets
+    copies = started(sources, targets, arrived)
+    place = lax.axis_index("ctx")
     requests, slots, page_rows = q_ref.shape[0], k_ref.shape[1], k_ref.shape[2]
     span = table.shape[1]
     positions = slots * page_rows
     heads[...] = jnp.zeros_like(heads)
+    for copy in copies[:3]:
+        copy.wait()
     queries = q_ref[...].astype(F32)
     for r in range(requests):
         for h in range(HEADS):
@@ -85,15 +103,15 @@
     for r in range(requests):
         seen = None
         for s in range(span):
-            position = (s * n_ctx + place[0]) * page_rows + offset
+            position = (s * n_ctx + place) * page_rows + offset
             here = (slot == table[r, s]) & (position < lengths[r])
             seen = here if seen is None else seen | here
         live = seen if live is None else jnp.where(row_id < r * GROUP, live.astype(jnp.int32), seen.astype(jnp.int32)) > 0
     out_row = lax.broadcasted_iota(jnp.int32, (ROWS, LANES), 0)
     diagonal = out_row == lax.broadcasted_iota(jnp.int32, (ROWS, LANES), 1)
     live = jnp.concatenate([live] * KV_HEADS, axis=0)
+    copies[3].wait()
     keys = k_ref[0].reshape(positions, KV_HEADS * HEAD_DIM)
-    values = v_ref[0].reshape(positions, KV_HEADS * HEAD_DIM)
     query = heads[...].astype(BF16)
 
     def rows(k):
@@ -121,6 +139,8 @@
     high = weights.astype(BF16)
     low = (weights - high.astype(F32)).astype(BF16)
     used = requests * GROUP
+    copies[4].wait()
+    values = v_ref[0].reshape(positions, KV_HEADS * HEAD_DIM)
     for k in range(KV_HEADS):
         mixes = jnp.dot(
             jnp.concatenate([high[rows(k)], low[rows(k)]], axis=0),
@@ -133,33 +153,32 @@
         out_ref[k] = jnp.where(
             out_row < used, mixes, jnp.where(out_row == used, top_row, total_row)
         )
-
-
-def attention_parts(
-    queries, key_pages, value_pages, block_table, lengths, residual, place, n_ctx
-):
-    smem = pl.BlockSpec(memory_space=pltpu.SMEM)
+    copies[5].wait()
+    width = own_ref.shape[1]
+    own_ref[...] = residual_ref[:, pl.ds(pl.multiple_of(place * width, width), width)]
+
+
+def attention_parts(queries, key_pages, value_pages, block_table, lengths, residual, n_ctx):
     vmem = pl.BlockSpec(memory_space=pltpu.VMEM)
+    scalars, arrays = (block_table, lengths), (queries, key_pages, value_pages, residual)
     return pl.pallas_call(
         functools.partial(attention_kernel, n_ctx),
         out_shape=(
             pltpu.VMEM((KV_HEADS, ROWS, HEAD_DIM), F32),
             pltpu.VMEM((residual.shape[0], residual.shape[1] // n_ctx), BF16),
         ),
-        in_specs=[smem, smem, smem, vmem, vmem, vmem, vmem],
+        in_specs=[pl.BlockSpec(memory_space=pltpu.HBM)] * 6,
         out_specs=(vmem, vmem),
-        scratch_shapes=[pltpu.VMEM((KV_HEADS * ROWS, HEAD_DIM), F32)],
+        scratch_shapes=[pltpu.VMEM((KV_HEADS * ROWS, HEAD_DIM), F32)]
+        + [pltpu.SMEM(x.shape, x.dtype) for x in scalars]
+        + [pltpu.VMEM(x.shape, x.dtype) for x in arrays]
+        + [pltpu.SemaphoreType.DMA((6,))],
         compiler_params=pltpu.CompilerParams(vmem_limit_bytes=KERNEL_VMEM),
         name="attention_parts",
-    )(
-        in_hbm(block_table),
-        in_hbm(lengths),
-        place,
-        *(in_hbm(x) for x in (queries, key_pages, value_pages, residual)),
-    )
-
-
-def merge_kernel(place, parts_ref, residual_ref, gain_ref, piece_ref, stream_ref, merged):
+    )(*(in_hbm(x) for x in scalars + arrays))
+
+
+def merge_kernel(parts_ref, residual_ref, gain_ref, piece_ref, stream_ref, merged):
     n_src, kv_here = parts_ref.shape[0], parts_ref.shape[1]
     requests, width = stream_ref.shape
     used = requests * GROUP
@@ -182,7 +201,7 @@
             for g in range(GROUP):
                 at = (k * GROUP + g) * HEAD_DIM
                 merged[r : r + 1, at : at + HEAD_DIM] = mixes[r * GROUP + g : r * GROUP + g + 1, :]
-    columns = pl.ds(pl.multiple_of(place[0] * width, width), width)
+    columns = pl.ds(pl.multiple_of(lax.axis_index("ctx") * width, width), width)
     stream = (residual_ref[...].astype(F32) + merged[...]).astype(BF16)
     stream_ref[...] = stream
     wide = stream.astype(F32)
@@ -201,9 +220,8 @@
         piece_ref[copy, :, width:] = spread
 
 
-def merge_parts(parts, residual, gain, place, width, copies):
+def merge_parts(parts, residual, gain, width, copies):
     requests = residual.shape[0]
-    smem = pl.BlockSpec(memory_space=pltpu.SMEM)
     vmem = pl.BlockSpec(memory_space=pltpu.VMEM)
     return pl.pallas_call(
         merge_kernel,
@@ -211,12 +229,12 @@
             pltpu.VMEM((copies, requests, width + LANES), BF16),
             jax.ShapeDtypeStruct((requests, width), BF16),
         ),
-        in_specs=[smem, vmem, vmem, vmem],
+        in_specs=[vmem, vmem, vmem],
         out_specs=(vmem, vmem),
         scratch_shapes=[pltpu.VMEM((requests, width), F32)],
         compiler_params=pltpu.CompilerParams(vmem_limit_bytes=KERNEL_VMEM),
         name="merge_parts",
-    )(place, in_vmem(parts), in_vmem(residual), gain)
+    )(in_vmem(parts), in_vmem(residual), gain)
 
 
 def row_shares(table, blocks, core, n_req, rows):
@@ -247,20 +265,19 @@
     return [picked[i : i + 1] + picked[i + 1 : i + 2] + picked[i + 2 : i + 3] for i in (0, 3)]
 
 
-def expert_kernel(model_width, n_req, exp_index, block_expert, tokens_ref, table_ref, *refs):
-    sources, out_ref, held, arrived = refs[:6], refs[6], refs[7:13], refs[13]
-    copies = [
-        pltpu.make_async_copy(source, here, arrived.at[i])
-        for i, (source, here) in enumerate(zip(sources, held))
-    ]
-    for copy in copies:
-        copy.start()
+def expert_kernel(model_width, n_req, block_source, table_source, tokens_ref, *refs):
+    sources, out_ref, held, block_expert, table_ref, turned, arrived = refs[:6], refs[6], refs[7:13], *refs[13:]
+    sources, targets = (block_source, table_source) + sources, (block_expert, table_ref) + held
+    copies = started(sources, targets, arrived)
+    for copy in copies[:2]:
+        copy.wait()
+    copies = copies[2:]
     n_xl, quarters, n_xh, far_rows, width = out_ref.shape
     n_ctx, rows, hidden = n_xl * n_xh, quarters * far_rows, held[0].shape[1]
     contract = (((1,), (1,)), ((), ()))
     ones = jnp.ones((8, LANES), BF16)
 
-    own = exp_index[0]
+    own = lax.axis_index("exp")
     core = lax.rem(own, 2)
     blocks = (block_expert[own], block_expert[own + 1 - 2 * core])
     shares = row_shares(table_ref[...], blocks, core, n_req, rows)
@@ -280,19 +297,20 @@
             squares, lax.dot_general(ones, tokens, contract, preferred_element_type=F32)
         )
     scale = lax.rsqrt(squares[:1] / model_width + EPSILON)
+    for chunk in range(n_ctx):
+        xl, xh = at(chunk)
+        tokens = tokens_ref[xl, :, xh, :, :width].reshape(rows, width)
+        turned[chunk] = tokens.T
     active = []
     for b in range(2):
         for copy in copies[2 * b : 2 * b + 2]:
             copy.wait()
         products = None
         for chunk in range(n_ctx):
-            xl, xh = at(chunk)
-            tokens = tokens_ref[xl, :, xh, :, :width].reshape(rows, width)
             columns = slice(chunk * width, (chunk + 1) * width)
             wide = jnp.concatenate([w[0, :, columns] for w in held[2 * b : 2 * b + 2]], axis=0)
             products = added(
-                products,
-                lax.dot_general(wide, tokens, contract, preferred_element_type=F32),
+                products, jnp.dot(wide, turned[chunk], preferred_element_type=F32)
             )
         gate, up = products[:hidden] * scale, products[hidden:] * scale
         active.append(gate / (1.0 + jnp.exp(-gate)) * up * shares[b])
@@ -314,21 +332,25 @@
     return table.transpose(2, 0, 1).reshape(2 * top, -1)
 
 
-def expert_partials(tokens, table, block_expert, weights, exp_index, n_req):
+def expert_partials(tokens, table, block_expert, weights, n_req):
     n_xl, quarters, n_xh, far_rows, padded = tokens.shape
     width = padded - LANES
     rows, model_width = quarters * far_rows, width * n_xl * n_xh
     hidden = weights[0].shape[1]
-    smem = pl.BlockSpec(memory_space=pltpu.SMEM)
+    hbm = pl.BlockSpec(memory_space=pltpu.HBM)
     vmem = pl.BlockSpec(memory_space=pltpu.VMEM)
     return pl.pallas_call(
         functools.partial(expert_kernel, float(model_width), n_req),
         out_shape=pltpu.VMEM((n_xl, quarters, n_xh, far_rows, width), BF16),
-        in_specs=[smem, smem, vmem, vmem]
-        + [pl.BlockSpec(memory_space=pltpu.HBM)] * len(weights),
+        in_specs=[hbm, hbm, vmem] + [hbm] * len(weights),
         out_specs=vmem,
         scratch_shapes=[pltpu.VMEM(w.shape, w.dtype) for w in weights]
-        + [pltpu.SemaphoreType.DMA((len(weights),))],
+        + [
+            pltpu.SMEM(block_expert.shape, block_expert.dtype),
+            pltpu.VMEM(table.shape, table.dtype),
+            pltpu.VMEM((n_xl * n_xh, width, rows), BF16),
+            pltpu.SemaphoreType.DMA((len(weights) + 2,)),
+        ],
         compiler_params=pltpu.CompilerParams(vmem_limit_bytes=KERNEL_VMEM),
         cost_estimate=pl.CostEstimate(
             flops=12 * rows * hidden * model_width,
@@ -337,7 +359,7 @@
         ),
         name="expert_partials",
     )(
-        exp_index, block_expert, in_vmem(tokens), in_vmem(table), *(in_hbm(w) for w in weights)
+        in_hbm(block_expert), in_hbm(table), in_vmem(tokens), *(in_hbm(w) for w in weights)
     )
 
 
@@ -361,8 +383,6 @@
     n_req, n_ctx, n_exp = (lax.axis_size(a) for a in AXES)
     requests, model_width = queries.shape
     width = model_width // n_ctx
-    place = lax.axis_index("ctx")
-    exp_index = lax.axis_index("exp")
     n_near, n_far = len(near[0]), len(far[0])
     far_rows = n_far // 2 * requests
 
@@ -378,13 +398,12 @@
         block_table,
         context_lengths,
         residual,
-        place[None],
         n_ctx,
     )
     parts = parts.reshape(n_ctx, KV_HEADS // n_ctx, ROWS, HEAD_DIM)
     parts = lax.all_to_all(parts, "ctx", 0, 0, tiled=True)
     piece, stream = merge_parts(
-        parts, residual, norm_gain.reshape(1, model_width), place[None], width, n_far
+        parts, residual, norm_gain.reshape(1, model_width), width, n_far
     )
 
     def exchange(x, groups):
@@ -399,7 +418,6 @@
         routing_table(expert_routes, route_weights),
         block_expert,
         (gate_blocks, up_blocks, gate_other, up_other, down_blocks, down_other),
-        exp_index[None],
         n_req,
     )
     partials = exchange(partials.reshape(n_near, 2, far_rows, width), near)

time: 109 us -> 107 us (0.982)
  Pallas kernels: 8.24 us -> 6.65 us
    pallas_call x1, Pallas kernels: 5.71 us -> 3.97 us  [expert_partials(): pl.pallas_call(functools.partial(expert_kernel, float(model_width), n_req...]
where the time goes in v3:
time: 107 us
  blocking collectives  71.9 us (67%)
  starting transfers between devices  17 us (16%)
  waiting for transfers between devices  7 us (7%)
  Pallas kernels  6.65 us (6%)
  local copies, waits for them, and re-layouts  2.97 us (3%)
    all_to_all x3, blocking collectives, exchange(): return lax.all_to_all(x, AXES, 0, 0, axis_index_groups=groups, tiled=True)  71.9 us
    all_to_all x1, starting transfers between devices, exchange(): return lax.all_to_all(x, AXES, 0, 0, axis_index_groups=groups, tiled=True)  6.53 us
    ppermute x3, starting transfers between devices, on_device(): lax.ppermute(w, 'exp', swap)  6.24 us
    all_to_all x1, starting transfers between devices, on_device(): parts = lax.all_to_all(parts, 'ctx', 0, 0, tiled=True)  4.28 us
    pallas_call x1, Pallas kernels, expert_partials(): pl.pallas_call(functools.partial(expert_kernel, float(model_width), n_req...  3.97 us
    all_to_all x1, waiting for transfers between devices, on_device(): parts = lax.all_to_all(parts, 'ctx', 0, 0, tiled=True)  2.57 us
    pallas_call x1, Pallas kernels, attention_parts(): pl.pallas_call(functools.partial(attention_kernel, n_ctx), out_shape=(plt...  2.44 us
    ppermute x3, waiting for transfers between devices, on_device(): lax.ppermute(w, 'exp', swap)  2.38 us
  transfers between devices with their start and end apart: 5, of which 4 were waited for; matrix products, arithmetic and copies ran while one was open for 1% of the time, Pallas kernels for 0%

profile of v3, /device:TPU:3, one launch (start us, length us, event | category | flops | bytes accessed | tf_op | source)
XLA Modules:
  0.0 106.5 jit_solution(5019580528686412306)
XLA Ops:
  0.0 2.4 %attention_parts.1 = (f32[8,16,128]{2,1,0:T(8,128)}, bf16[2,1536]{1,0:T(2,128)(2,1)S(1)}) custom-call(s32[2,2]{1,0:T(2,128)} %refs_0_.2, s32[2]{0:T(128)} %refs_1_.2, bf16[2,6144]{1,0:T(2,128)(2,1)} %refs_2_.1, bf16[1,3,64,1024]{3,2,1,0:T(8,128)(2,1)} %refs_3_.1, bf16[1,3,64,1024]{3,2,1,0:T(8,128)(2,1)} %refs_4_.2, bf16[2,6144]{1,0:T(2,128)(2,1)} %refs_5_.1), custom_call_target="tpu_custom_call" | custom-call | tf_op jit(solution)/shard_map/attention_parts/pallas_call | solution.py:164
  2.5 4.3 %all-to-all-start = ((f32[4,2,16,128]{3,2,1,0:T(8,128)}), f32[4,2,16,128]{3,2,1,0:T(8,128)S(1)}, u32[]{:S(2)}, u32[]{:S(2)}) async-start(f32[4,2,16,128]{3,2,1,0:T(8,128)} %bitcast), calls=%async_computation | async-start | bytes 131072 | tf_op jit(solution)/shard_map/all_to_all | solution.py:404
  6.7 0.7 reshape.22.gain_ref
  7.5 2.6 %all-to-all-done.parts_ref = f32[4,2,16,128]{3,2,1,0:T(8,128)S(1)} async-done(((f32[4,2,16,128]{3,2,1,0:T(8,128)}), f32[4,2,16,128]{3,2,1,0:T(8,128)S(1)}, u32[]{:S(2)}, u32[]{:S(2)}) %all-to-all-start) | async-done | bytes 65568 | tf_op jit(solution)/shard_map/all_to_all | solution.py:404
  10.0 0.2 merge_parts.1
  10.3 32.0 %all_to_all.25 = bf16[32,2,1664]{2,1,0:T(2,128)(2,1)S(1)} all-to-all(bf16[32,2,1664]{2,1,0:T(2,128)(2,1)S(1)} %get-tuple-element.12), channel_id=1, replica_groups={{0,4,8,12,128,132,136,140,256,260,264,268,384,388,392,396,32,36,40,44,1..., dimensions={0} | all-to-all | bytes 425984 | tf_op jit(solution)/shard_map/all_to_all | solution.py:410
  42.3 0.1 reshape.24
  42.4 1.4 %broadcast_in_dim.3 = bf16[8,2,32,1664]{3,2,1,0:T(8,128)(2,1)} broadcast(bf16[2,32,1664]{2,1,0:T(8,128)(2,1)S(1)} %reshape.24), dimensions={1,2,3} | broadcast | bytes 1916928 | tf_op jit(solution)/shard_map/broadcast_in_dim | solution.py:414
  43.8 0.0 copy-start
  43.8 0.0 copy-start.1
  43.8 0.0 copy-start.2
  43.8 6.5 %all-to-all-start.2 = ((bf16[8,2,32,1664]{3,2,1,0:T(8,128)(2,1)}), bf16[8,2,32,1664]{3,2,1,0:T(8,128)(2,1)S(1)}, u32[]{:S(2)}, u32[]{:S(2)}) async-start(bf16[8,2,32,1664]{3,2,1,0:T(8,128)(2,1)} %broadcast_in_dim.3), calls=%async_computation.2 | async-start | bytes 3407872 | tf_op jit(solution)/shard_map/all_to_all | solution.py:410
  50.3 0.0 copy-done
  50.3 1.9 %collective-permute-start = (bf16[1,96,6144]{2,1,0:T(8,128)(2,1)S(1)}, bf16[1,96,6144]{2,1,0:T(8,128)(2,1)}, u32[]{:S(2)}, u32[]{:S(2)}) collective-permute-start(bf16[1,96,6144]{2,1,0:T(8,128)(2,1)S(1)} %copy-done), channel_id=1, source_target_pairs={{0,1},{1,0},{2,3},{3,2},{4,5},{5,4},{6,7},{7,6},{8,9},{9,8},{10,11... | collective-permute-start | bytes 3538952 | tf_op jit(solution)/shard_map/ppermute | solution.py:391
  52.2 2.4 %collective-permute-start.1 = (bf16[1,96,6144]{2,1,0:T(8,128)(2,1)}, bf16[1,96,6144]{2,1,0:T(8,128)(2,1)}, u32[]{:S(2)}, u32[]{:S(2)}) collective-permute-start(bf16[1,96,6144]{2,1,0:T(8,128)(2,1)} %refs_1_.3), channel_id=1, source_target_pairs={{0,1},{1,0},{2,3},{3,2},{4,5},{5,4},{6,7},{7,6},{8,9},{9,8},{10,11... | collective-permute-start | bytes 3538952 | tf_op jit(solution)/shard_map/ppermute | solution.py:391
  54.6 1.9 %collective-permute-start.2 = (bf16[1,96,6144]{2,1,0:T(8,128)(2,1)}, bf16[1,96,6144]{2,1,0:T(8,128)(2,1)}, u32[]{:S(2)}, u32[]{:S(2)}) collective-permute-start(bf16[1,96,6144]{2,1,0:T(8,128)(2,1)} %refs_4_.3), channel_id=1, source_target_pairs={{0,1},{1,0},{2,3},{3,2},{4,5},{5,4},{6,7},{7,6},{8,9},{9,8},{10,11... | collective-permute-start | bytes 3538952 | tf_op jit(solution)/shard_map/ppermute | solution.py:391
  56.6 0.0 copy-done.1
  56.6 0.0 copy-done.2
  56.7 0.7 reshape.23.table_source
  57.3 0.0 collective-permute-done.refs_2_
  57.3 0.1 collective-permute-done.1.refs_3_
  57.4 2.3 %collective-permute-done.2.refs_5_ = bf16[1,96,6144]{2,1,0:T(8,128)(2,1)} collective-permute-done((bf16[1,96,6144]{2,1,0:T(8,128)(2,1)}, bf16[1,96,6144]{2,1,0:T(8,128)(2,1)}, u32[]{:S(2)}, u32[]{:S(2)}) %collective-permute-start.2) | collective-permute-done | bytes 1179680 | tf_op jit(solution)/shard_map/ppermute | solution.py:391
  59.7 2.0 %all-to-all-done.2 = bf16[8,2,32,1664]{3,2,1,0:T(8,128)(2,1)S(1)} async-done(((bf16[8,2,32,1664]{3,2,1,0:T(8,128)(2,1)}), bf16[8,2,32,1664]{3,2,1,0:T(8,128)(2,1)S(1)}, u32[]{:S(2)}, u32[]{:S(2)}) %all-to-all-start.2) | async-done | bytes 1703968 | tf_op jit(solution)/shard_map/all_to_all | solution.py:410
  61.8 4.0 %expert_partials.1 = bf16[2,4,2,32,1536]{4,3,2,1,0:T(8,128)(2,1)S(1)} custom-call(s32[16]{0:T(128)} %block_source.1, f32[8,256]{1,0:T(8,128)} %reshape.23.table_source, bf16[2,4,2,32,1664]{4,3,2,1,0:T(8,128)(2,1)S(1)} %bitcast.5, bf16[1,96,6144]{2,1,0:T(8,128)(2,1)} %refs_0_.3, bf16[1,96,6144]{2,1,0:T(8,128)(2,1)} %refs_1_.3, ...), custom_call_target="tpu_custom_call" | custom-call | flops 905969664 | bytes 7077888 | tf_op jit(solution)/shard_map/expert_partials/pallas_call | solution.py:342
  65.8 17.7 %all_to_all.26 = bf16[8,2,32,1536]{3,2,1,0:T(8,128)(2,1)S(1)} all-to-all(bf16[8,2,32,1536]{3,2,1,0:T(8,128)(2,1)S(1)} %bitcast.6), channel_id=1, replica_groups={{0,2,64,66,16,18,80,82},{4,6,68,70,20,22,84,86},{8,10,72,74,24,26,88,90..., dimensions={0} | all-to-all | bytes 3145728 | tf_op jit(solution)/shard_map/all_to_all | solution.py:410
  83.5 0.2 reduce_sum.21
  83.7 0.1 reshape.27
  83.8 22.1 %all_to_all.27 = bf16[32,2,1536]{2,1,0:T(2,128)(2,1)S(1)} all-to-all(bf16[32,2,1536]{2,1,0:T(2,128)(2,1)S(1)} %reshape.27), channel_id=1, replica_groups={{0,4,8,12,128,132,136,140,256,260,264,268,384,388,392,396,32,36,40,44,1..., dimensions={0} | all-to-all | bytes 393216 | tf_op jit(solution)/shard_map/all_to_all | solution.py:410
  105.9 0.6 add_convert_fusion
  (4 shorter events, 0.1 us)
Async XLA Ops:
  2.5 7.6 %all-to-all-start = ((f32[4,2,16,128]{3,2,1,0:T(8,128)}), f32[4,2,16,128]{3,2,1,0:T(8,128)S(1)}, u32[]{:S(2)}, u32[]{:S(2)}) async-start(f32[4,2,16,128]{3,2,1,0:T(8,128)} %bitcast), calls=%async_computation | async-start | bytes 131072 | tf_op jit(solution)/shard_map/all_to_all | solution.py:404
  43.8 6.5 %copy-start = (bf16[1,96,6144]{2,1,0:T(8,128)(2,1)S(1)}, bf16[1,96,6144]{2,1,0:T(8,128)(2,1)}, u32[]{:S(2)}) copy-start(bf16[1,96,6144]{2,1,0:T(8,128)(2,1)} %refs_0_.3) | copy-start | bytes 3538948
  43.8 12.8 %copy-start.1 = (s32[16,16,4]{1,2,0:T(4,128)S(1)}, s32[16,16,4]{1,2,0:T(4,128)}, u32[]{:S(2)}) copy-start(s32[16,16,4]{1,2,0:T(4,128)} %param.23) | copy-start | bytes 12292
  43.8 12.8 %copy-start.2 = (f32[16,16,4]{1,2,0:T(4,128)S(1)}, f32[16,16,4]{1,2,0:T(4,128)}, u32[]{:S(2)}) copy-start(f32[16,16,4]{1,2,0:T(4,128)} %param.24) | copy-start | bytes 12292
  43.8 18.0 %all-to-all-start.2 = ((bf16[8,2,32,1664]{3,2,1,0:T(8,128)(2,1)}), bf16[8,2,32,1664]{3,2,1,0:T(8,128)(2,1)S(1)}, u32[]{:S(2)}, u32[]{:S(2)}) async-start(bf16[8,2,32,1664]{3,2,1,0:T(8,128)(2,1)} %broadcast_in_dim.3), calls=%async_computation.2 | async-start | bytes 3407872 | tf_op jit(solution)/shard_map/all_to_all | solution.py:410
  50.3 7.0 %collective-permute-start = (bf16[1,96,6144]{2,1,0:T(8,128)(2,1)S(1)}, bf16[1,96,6144]{2,1,0:T(8,128)(2,1)}, u32[]{:S(2)}, u32[]{:S(2)}) collective-permute-start(bf16[1,96,6144]{2,1,0:T(8,128)(2,1)S(1)} %copy-done), channel_id=1, source_target_pairs={{0,1},{1,0},{2,3},{3,2},{4,5},{5,4},{6,7},{7,6},{8,9},{9,8},{10,11... | collective-permute-start | bytes 3538952 | tf_op jit(solution)/shard_map/ppermute | solution.py:391
  52.2 5.2 %collective-permute-start.1 = (bf16[1,96,6144]{2,1,0:T(8,128)(2,1)}, bf16[1,96,6144]{2,1,0:T(8,128)(2,1)}, u32[]{:S(2)}, u32[]{:S(2)}) collective-permute-start(bf16[1,96,6144]{2,1,0:T(8,128)(2,1)} %refs_1_.3), channel_id=1, source_target_pairs={{0,1},{1,0},{2,3},{3,2},{4,5},{5,4},{6,7},{7,6},{8,9},{9,8},{10,11... | collective-permute-start | bytes 3538952 | tf_op jit(solution)/shard_map/ppermute | solution.py:391
  54.6 5.1 %collective-permute-start.2 = (bf16[1,96,6144]{2,1,0:T(8,128)(2,1)}, bf16[1,96,6144]{2,1,0:T(8,128)(2,1)}, u32[]{:S(2)}, u32[]{:S(2)}) collective-permute-start(bf16[1,96,6144]{2,1,0:T(8,128)(2,1)} %refs_4_.3), channel_id=1, source_target_pairs={{0,1},{1,0},{2,3},{3,2},{4,5},{5,4},{6,7},{7,6},{8,9},{9,8},{10,11... | collective-permute-start | bytes 3538952 | tf_op jit(solution)/shard_map/ppermute | solution.py:391

commit v4 on v3

v4 whole, which is shorter than its diff:
```python
import functools

import jax
import jax.numpy as jnp
import numpy as np
from jax import lax
from jax.experimental import pallas as pl
from jax.experimental.pallas import tpu as pltpu
from jax.sharding import PartitionSpec as P

HEADS = 48
KV_HEADS = 8
HEAD_DIM = 128
GROUP = HEADS // KV_HEADS
EPSILON = 1e-05
NEGATIVE = -1e30
ROWS = 16
LANES = 128
KERNEL_VMEM = 16 << 20
AXES = ("req", "ctx", "exp")
F32 = jnp.float32
BF16 = jnp.bfloat16


def in_vmem(x):
    return pltpu.with_memory_space_constraint(x, pltpu.VMEM)


def in_hbm(x):
    return pltpu.with_memory_space_constraint(x, pltpu.HBM)


def exchange_groups(n_req, n_ctx, n_exp):
    cols = n_exp // 2

    def device(z, x, y, core):
        z, x, y = (z + core) % n_req, (x + core) % n_ctx, (y + core) % cols
        return (z * n_ctx + x) * n_exp + y * 2 + core

    near = [
        [
            device(2 * zh + zl, 2 * xh + xl, 2 * yh + yl, core)
            for xl in (0, 1)
            for zl in (0, 1)
            for yl in (0, 1)
        ]
        for core in (0, 1)
        for xh in range(n_ctx // 2)
        for zh in range(n_req // 2)
        for yh in range(cols // 2)
    ]
    far = [
        [
            device(2 * zh + zl, 2 * xh + xl, 2 * yh + yl, core)
            for xh in range(n_ctx // 2)
            for zh in range(n_req // 2)
            for yh in range(cols // 2)
        ]
        for core in (0, 1)
        for xl in (0, 1)
        for zl in (0, 1)
        for yl in (0, 1)
    ]
    columns_far = [
        [
            device(2 * zh + zl, x, 2 * yh + yl, core)
            for zh in range(n_req // 2)
            for yh in range(cols // 2)
        ]
        for core in (0, 1)
        for x in range(n_ctx)
        for zl in (0, 1)
        for yl in (0, 1)
    ]
    return near, far, columns_far


def started(sources, targets, arrived):
    copies = [
        pltpu.make_async_copy(source, target, arrived.at[i])
        for i, (source, target) in enumerate(zip(sources, targets))
    ]
    for copy in copies:
        copy.start()
    return copies


def attention_kernel(n_ctx, *refs):
    sources, (out_ref, own_ref, scale_ref), heads, gains, targets, arrived = (
        refs[:7],
        refs[7:10],
        refs[10],
        refs[11],
        refs[12:19],
        refs[19],
    )
    table, lengths, q_ref, k_ref, v_ref, residual_ref, gain_ref = targets
    copies = started(sources, targets, arrived)
    place = lax.axis_index("ctx")
    requests, slots, page_rows = q_ref.shape[0], k_ref.shape[1], k_ref.shape[2]
    span = table.shape[1]
    positions = slots * page_rows
    heads[...] = jnp.zeros_like(heads)
    for copy in copies[:3]:
        copy.wait()
    queries = q_ref[...].astype(F32)
    for r in range(requests):
        for h in range(HEADS):
            row = (h // GROUP) * ROWS + r * GROUP + h % GROUP
            heads[row : row + 1, :] = queries[r : r + 1, h * HEAD_DIM : (h + 1) * HEAD_DIM]
    at = lax.broadcasted_iota(jnp.int32, (ROWS, positions), 1)
    row_id = lax.broadcasted_iota(jnp.int32, (ROWS, positions), 0)
    slot, offset = at // page_rows, at % page_rows
    live = None
    for r in range(requests):
        seen = None
        for s in range(span):
            position = (s * n_ctx + place) * page_rows + offset
            here = (slot == table[r, s]) & (position < lengths[r])
            seen = here if seen is None else seen | here
        live = seen if live is None else jnp.where(row_id < r * GROUP, live.astype(jnp.int32), seen.astype(jnp.int32)) > 0
    out_row = lax.broadcasted_iota(jnp.int32, (ROWS, LANES), 0)
    diagonal = out_row == lax.broadcasted_iota(jnp.int32, (ROWS, LANES), 1)
    live = jnp.concatenate([live] * KV_HEADS, axis=0)
    copies[3].wait()
    keys = k_ref[0].reshape(positions, KV_HEADS * HEAD_DIM)
    query = heads[...].astype(BF16)

    def rows(k):
        return slice(k * ROWS, (k + 1) * ROWS)

    def lanes(k):
        return slice(k * HEAD_DIM, (k + 1) * HEAD_DIM)

    scores = jnp.concatenate(
        [
            lax.dot_general(
                query[rows(k)],
                keys[:, lanes(k)],
                (((1,), (1,)), ((), ())),
                preferred_element_type=F32,
            )
            for k in range(KV_HEADS)
        ],
        axis=0,
    )
    scores = jnp.where(live, scores * HEAD_DIM ** (-0.5), NEGATIVE)
    top = jnp.max(scores, axis=1, keepdims=True)
    weights = jnp.where(live, jnp.exp(scores - top), 0.0)
    total = jnp.sum(weights, axis=1, keepdims=True)
    high = weights.astype(BF16)
    low = (weights - high.astype(F32)).astype(BF16)
    used = requests * GROUP
    copies[4].wait()
    values = v_ref[0].reshape(positions, KV_HEADS * HEAD_DIM)
    for k in range(KV_HEADS):
        mixes = jnp.dot(
            jnp.concatenate([high[rows(k)], low[rows(k)]], axis=0),
            values[:, lanes(k)],
            preferred_element_type=F32,
        )
        mixes = mixes[:ROWS] + mixes[ROWS:]
        top_row = jnp.sum(jnp.where(diagonal, top[rows(k)], 0.0), axis=0, keepdims=True)
        total_row = jnp.sum(jnp.where(diagonal, total[rows(k)], 0.0), axis=0, keepdims=True)
        part = jnp.where(
            out_row < used, mixes, jnp.where(out_row == used, top_row, total_row)
        )
        chunk, k = divmod(k, KV_HEADS // n_ctx)
        out_ref[chunk, 0, k] = part
        out_ref[(chunk + n_ctx // 2) % n_ctx, 1, k] = part
    for copy in copies[5:]:
        copy.wait()
    gains[...] = gain_ref[...].astype(F32)
    width = own_ref.shape[2]
    for i in range(2):
        column = lax.rem(place + i * (n_ctx // 2), n_ctx)
        own_ref[i] = residual_ref[:, pl.ds(pl.multiple_of(column * width, width), width)]
        for h in range(width // LANES):
            row = gains[pl.ds(column * (width // LANES) + h, 1), :]
            scale_ref[i, :, h * LANES : (h + 1) * LANES] = row


def attention_parts(
    queries, key_pages, value_pages, block_table, lengths, residual, gain, n_ctx
):
    vmem = pl.BlockSpec(memory_space=pltpu.VMEM)
    scalars, arrays = (block_table, lengths), (queries, key_pages, value_pages, residual, gain)
    return pl.pallas_call(
        functools.partial(attention_kernel, n_ctx),
        out_shape=(
            pltpu.VMEM((n_ctx, 2, KV_HEADS // n_ctx, ROWS, HEAD_DIM), F32),
            pltpu.VMEM((2, residual.shape[0], residual.shape[1] // n_ctx), BF16),
            pltpu.VMEM((2, 1, residual.shape[1] // n_ctx), F32),
        ),
        in_specs=[pl.BlockSpec(memory_space=pltpu.HBM)] * 7,
        out_specs=(vmem, vmem, vmem),
        scratch_shapes=[pltpu.VMEM((KV_HEADS * ROWS, HEAD_DIM), F32), pltpu.VMEM(gain.shape, F32)]
        + [pltpu.SMEM(x.shape, x.dtype) for x in scalars]
        + [pltpu.VMEM(x.shape, x.dtype) for x in arrays]
        + [pltpu.SemaphoreType.DMA((7,))],
        compiler_params=pltpu.CompilerParams(vmem_limit_bytes=KERNEL_VMEM),
        name="attention_parts",
    )(*(in_hbm(x) for x in scalars + arrays))


def merge_kernel(parts_ref, residual_ref, gain_ref, piece_ref, stream_ref, merged):
    n_src, kv_here = parts_ref.shape[0], parts_ref.shape[2]
    requests, width = stream_ref.shape
    used = requests * GROUP
    place = lax.axis_index("ctx")
    core = lax.rem(lax.axis_index("exp"), 2)
    diagonal = lax.broadcasted_iota(jnp.int32, (ROWS, LANES), 0) == lax.broadcasted_iota(
        jnp.int32, (ROWS, LANES), 1
    )

    def column(row):
        return jnp.sum(jnp.where(diagonal, row, 0.0), axis=1, keepdims=True)

    scaled, square = [], 0.0
    for i in range(2):
        for k in range(kv_here):
            tops = [column(parts_ref[s, i, k, used : used + 1, :]) for s in range(n_src)]
            totals = [column(parts_ref[s, i, k, used + 1 : used + 2, :]) for s in range(n_src)]
            top = functools.reduce(jnp.maximum, tops)
            scales = [jnp.exp(t - top) for t in tops]
            mixes = sum(parts_ref[s, i, k] * scales[s] for s in range(n_src))
            total = sum(totals[s] * scales[s] for s in range(n_src))
            mixes = mixes / total
            for r in range(requests):
                for g in range(GROUP):
                    at = (k * GROUP + g) * HEAD_DIM
                    row = r * GROUP + g
                    merged[i, r : r + 1, at : at + HEAD_DIM] = mixes[row : row + 1, :]
        stream = (residual_ref[i].astype(F32) + merged[i]).astype(BF16)
        if i == 0:
            stream_ref[...] = stream
        wide = stream.astype(F32)
        scaled.append(wide * gain_ref[i])
        square += jnp.sum(wide * wide, axis=1, keepdims=True)
    first = square.astype(BF16).astype(F32)
    second = (square - first).astype(BF16).astype(F32)
    third = square - first - second
    lane = lax.broadcasted_iota(jnp.int32, (requests, LANES), 1)
    spread = jnp.where(
        lane == 0, first, jnp.where(lane == 1, second, jnp.where(lane == 2, third, 0.0))
    ).astype(BF16)
    upper = lax.rem(place - core + n_src, n_src) >= n_src // 2
    low = jnp.where(upper, scaled[1], scaled[0]).astype(BF16)
    high = jnp.where(upper, scaled[0], scaled[1]).astype(BF16)
    for copy in range(piece_ref.shape[0]):
        piece_ref[copy, :, :width] = low
        piece_ref[copy, :, width : 2 * width] = high
        piece_ref[copy, :, 2 * width :] = spread


def merge_parts(parts, residual, gain, copies):
    _, requests, width = residual.shape
    vmem = pl.BlockSpec(memory_space=pltpu.VMEM)
    return pl.pallas_call(
        merge_kernel,
        out_shape=(
            pltpu.VMEM((copies, requests, 2 * width + LANES), BF16),
            jax.ShapeDtypeStruct((requests, width), BF16),
        ),
        in_specs=[vmem, vmem, vmem],
        out_specs=(vmem, vmem),
        scratch_shapes=[pltpu.VMEM((2, requests, width), F32)],
        compiler_params=pltpu.CompilerParams(vmem_limit_bytes=KERNEL_VMEM),
        name="merge_parts",
    )(in_vmem(parts), in_vmem(residual), in_vmem(gain))


def row_shares(routes_ref, weights_ref, blocks, core, requests, rows):
    n_exp, _, entries = routes_ref.shape
    n_req, half_y = entries // requests, n_exp // 4
    row = lax.broadcasted_iota(jnp.int32, (entries, rows), 1)
    entry = lax.broadcasted_iota(jnp.int32, (entries, rows), 0)
    request, row = row % requests, row // requests
    yh, row = row % half_y, row // half_y
    zh, row = row % (n_req // 2), row // (n_req // 2)
    yl, zl = row % 2, row // 2
    here = entry == (2 * zh + zl + core) % n_req * requests + request
    y = (2 * yh + yl + core) % (n_exp // 2)
    diagonal = lax.broadcasted_iota(jnp.int32, (entries, entries), 0) == lax.broadcasted_iota(
        jnp.int32, (entries, entries), 1
    )
    shares = [jnp.zeros((entries, rows), F32) for _ in blocks]
    for column in range(n_exp // 2):
        routes, weights = routes_ref[2 * column + core], weights_ref[2 * column + core]
        at = here & (y == column)
        for b, block in enumerate(blocks):
            line = jnp.sum(jnp.where(routes == block, weights, 0.0), axis=0, keepdims=True)
            upright = jnp.sum(jnp.where(diagonal, line, 0.0), axis=1, keepdims=True)
            shares[b] += jnp.where(at, upright, 0.0)
    return [jnp.sum(share, axis=0, keepdims=True) for share in shares]


def expert_kernel(model_width, requests, block_source, route_source, weight_source, tokens_ref, *refs):
    sources, gate_held, out_ref, held = refs[:5], refs[5], refs[6], refs[7:12]
    block_expert, routes_ref, weights_ref, turned, arrived = refs[12:]
    copies = started(
        (block_source, route_source, weight_source) + sources,
        (block_expert, routes_ref, weights_ref) + held,
        arrived,
    )
    held = (gate_held,) + held
    for copy in copies[:3]:
        copy.wait()
    copies = copies[3:]
    n_xl, quarters, n_xh, far_rows, width = out_ref.shape
    n_ctx, rows, hidden = n_xl * n_xh, quarters * far_rows, held[0].shape[1]
    contract = (((1,), (1,)), ((), ()))
    ones = jnp.ones((8, LANES), BF16)

    own = lax.axis_index("exp")
    core = lax.rem(own, 2)
    blocks = (block_expert[own + 1 - 2 * core], block_expert[own])
    shares = row_shares(routes_ref, weights_ref, blocks, core, requests, rows)

    def at(chunk):
        column = lax.rem(chunk + n_ctx - core, n_ctx)
        return column % n_xl, column // n_xl

    def added(total, term):
        return term if total is None else total + term

    squares = None
    for xl in range(n_xl):
        tokens = tokens_ref[xl, :, :, n_xh * width :].reshape(rows, LANES)
        squares = added(
            squares, lax.dot_general(ones, tokens, contract, preferred_element_type=F32)
        )
        for xh in range(n_xh):
            tokens = tokens_ref[xl, :, :, xh * width : (xh + 1) * width].reshape(rows, width)
            turned[lax.rem(xh * n_xl + xl + core, n_ctx)] = tokens.T
    scale = lax.rsqrt(squares[:1] / model_width + EPSILON)
    active = []
    for b in range(2):
        for copy in copies[1:3] if b else copies[:1]:
            copy.wait()
        products = None
        for chunk in range(n_ctx):
            columns = slice(chunk * width, (chunk + 1) * width)
            wide = jnp.concatenate([w[0, :, columns] for w in held[2 * b : 2 * b + 2]], axis=0)
            products = added(
                products, jnp.dot(wide, turned[chunk], preferred_element_type=F32)
            )
        gate, up = products[:hidden] * scale, products[hidden:] * scale
        active.append(gate / (1.0 + jnp.exp(-gate)) * up * shares[b])
    active.append(jnp.zeros((-2 * hidden % LANES, rows), F32))
    active = jnp.concatenate(active, axis=0).T[:, : 2 * hidden].astype(BF16)
    for copy in copies[3:]:
        copy.wait()
    for chunk in range(n_ctx):
        xl, xh = at(chunk)
        columns = slice(chunk * width, (chunk + 1) * width)
        down = jnp.concatenate([w[0, :, columns] for w in held[4:]], axis=0)
        total = jnp.dot(active, down, preferred_element_type=F32).astype(BF16)
        out_ref[xl, :, xh] = total.reshape(quarters, far_rows, width)


def expert_partials(
    tokens, routes, route_weights, block_expert, gate_other, weights, requests
):
    n_xl, quarters, far_rows, padded = tokens.shape
    n_xh = 2
    width = (padded - LANES) // n_xh
    rows, model_width = quarters * far_rows, width * n_xl * n_xh
    hidden = weights[0].shape[1]
    hbm = pl.BlockSpec(memory_space=pltpu.HBM)
    vmem = pl.BlockSpec(memory_space=pltpu.VMEM)
    return pl.pallas_call(
        functools.partial(expert_kernel, float(model_width), requests),
        out_shape=pltpu.VMEM((n_xl, quarters, n_xh, far_rows, width), BF16),
        in_specs=[hbm, hbm, hbm, vmem] + [hbm] * len(weights) + [vmem],
        out_specs=vmem,
        scratch_shapes=[pltpu.VMEM(w.shape, w.dtype) for w in weights]
        + [
            pltpu.SMEM(block_expert.shape, block_expert.dtype),
            pltpu.VMEM(routes.shape, routes.dtype),
            pltpu.VMEM(route_weights.shape, route_weights.dtype),
            pltpu.VMEM((n_xl * n_xh, width, rows), BF16),
            pltpu.SemaphoreType.DMA((len(weights) + 3,)),
        ],
        compiler_params=pltpu.CompilerParams(vmem_limit_bytes=KERNEL_VMEM),
        cost_estimate=pl.CostEstimate(
            flops=12 * rows * hidden * model_width,
            bytes_accessed=12 * hidden * model_width,
            transcendentals=0,
        ),
        name="expert_partials",
    )(
        *(in_hbm(x) for x in (block_expert, routes, route_weights)),
        in_vmem(tokens),
        *(in_hbm(w) for w in weights),
        in_vmem(gate_other),
    )


def on_device(
    groups,
    queries,
    key_pages,
    value_pages,
    block_table,
    context_lengths,
    residual,
    norm_gain,
    gate_blocks,
    up_blocks,
    down_blocks,
    expert_routes,
    route_weights,
    block_expert,
):
    near, far, columns_far = groups
    n_req, n_ctx, n_exp = (lax.axis_size(a) for a in AXES)
    requests, model_width = queries.shape
    width = model_width // n_ctx
    n_near, n_far = len(near[0]), len(far[0])
    far_rows = len(columns_far[0]) * requests

    swap = [(i, i ^ 1) for i in range(n_exp)]
    gate_other, up_other, down_other = (
        lax.ppermute(w, "exp", swap) for w in (gate_blocks, up_blocks, down_blocks)
    )

    parts, residual, gain = attention_parts(
        queries,
        key_pages,
        value_pages,
        block_table,
        context_lengths,
        residual,
        norm_gain.reshape(-1, LANES),
        n_ctx,
    )
    parts = lax.all_to_all(parts, "ctx", 0, 0, tiled=True)
    piece, stream = merge_parts(parts, residual, gain, len(columns_far[0]))

    def exchange(x, groups):
        return lax.all_to_all(x, AXES, 0, 0, axis_index_groups=groups, tiled=True)

    tokens = exchange(piece, columns_far)
    tokens = tokens.reshape(far_rows, piece.shape[2])
    tokens = exchange(jnp.broadcast_to(tokens, (n_near,) + tokens.shape), near)
    tokens = tokens.reshape(2, n_near // 2, far_rows, piece.shape[2])
    partials = expert_partials(
        tokens,
        expert_routes.transpose(0, 2, 1),
        route_weights.transpose(0, 2, 1),
        block_expert,
        gate_other,
        (up_other, gate_blocks, up_blocks, down_other, down_blocks),
        requests,
    )
    partials = exchange(partials.reshape(n_near, 2, far_rows, width), near)
    partials = jnp.sum(partials.astype(F32), axis=0).astype(BF16)
    partials = exchange(partials.reshape(n_far, requests, width), far)
    expert_sum = jnp.sum(partials.astype(F32), axis=0)
    return (stream.astype(F32) + expert_sum).astype(BF16)


def solution(mesh):
    in_specs = (
        P(("req", "exp"), None),
        P(("req", "exp"), "ctx", None, None),
        P(("req", "exp"), "ctx", None, None),
        P(("req", "exp"), "ctx"),
        P(("req", "exp")),
        P(("req", "exp"), None),
        P(),
        P("exp", ("req", "ctx"), None),
        P("exp", ("req", "ctx"), None),
        P("exp", ("req", "ctx"), None),
        P(),
        P(),
        P(),
    )
    out_specs = P(("req", "exp"), "ctx")
    groups = exchange_groups(*(mesh.shape[a] for a in AXES))
    return jax.shard_map(
        functools.partial(on_device, groups),
        mesh=mesh,
        in_specs=in_specs,
        out_specs=out_specs,
        check_vma=False,
    )
```

time: 107 us -> 104 us (0.972)
  blocking collectives: 71.9 us -> 77.8 us
  waiting for transfers between devices: 7 us -> 1.36 us
  starting transfers between devices: 17 us -> 14.3 us
    all_to_all x0 -> x1, blocking collectives: none -> 7.71 us  [on_device(): parts = lax.all_to_all(parts, 'ctx', 0, 0, tiled=True)]
    all_to_all x1 -> x0, starting transfers between devices: 4.28 us -> none  [on_device(): parts = lax.all_to_all(parts, 'ctx', 0, 0, tiled=True)]
    all_to_all x1 -> x0, waiting for transfers between devices: 2.57 us -> none  [on_device(): parts = lax.all_to_all(parts, 'ctx', 0, 0, tiled=True)]
    ppermute x3, starting transfers between devices: 6.24 us -> 8.27 us  [on_device(): lax.ppermute(w, 'exp', swap)]
    all_to_all x1, waiting for transfers between devices: 2.04 us -> 0.16 us  [exchange(): return lax.all_to_all(x, AXES, 0, 0, axis_index_groups=groups, tiled=True)]
    all_to_all x3, blocking collectives: 71.9 us -> 70.1 us  [exchange(): return lax.all_to_all(x, AXES, 0, 0, axis_index_groups=groups, tiled=True)]
    unnamed x6 -> x4, local copies, waits for them, and re-layouts: 0.01 us -> 1.45 us
    reshape x3 -> x1, local copies, waits for them, and re-layouts: 1.49 us -> 0.08 us  [on_device(): tokens = tokens.reshape(far_rows, piece.shape[2])]
  transfers between devices with their start and end apart: 5 -> 4, of which waited for: 4 -> 3; matrix products, arithmetic and copies ran while one was open for 1% -> 0% of each run, Pallas kernels for 0% -> 0%
where the time goes in v4:
time: 104 us; the launch traced here: 103 us
  blocking collectives  77.8 us (75%)
  starting transfers between devices  14.3 us (14%)
  Pallas kernels  5.8 us (6%)
  local copies, waits for them, and re-layouts  2.88 us (3%)
  waiting for transfers between devices  1.36 us (1%)
    all_to_all x3, blocking collectives, exchange(): return lax.all_to_all(x, AXES, 0, 0, axis_index_groups=groups, tiled=True)  70.1 us
    ppermute x3, starting transfers between devices, on_device(): lax.ppermute(w, 'exp', swap)  8.27 us
    all_to_all x1, blocking collectives, on_device(): parts = lax.all_to_all(parts, 'ctx', 0, 0, tiled=True)  7.71 us
    all_to_all x1, starting transfers between devices, exchange(): return lax.all_to_all(x, AXES, 0, 0, axis_index_groups=groups, tiled=True)  6.06 us
    pallas_call x1, Pallas kernels, expert_partials(): pl.pallas_call(functools.partial(expert_kernel, float(model_width), reque...  3.69 us
  transfers between devices with their start and end apart: 4, of which 3 were waited for; matrix products, arithmetic and copies ran while one was open for 0% of the time, Pallas kernels for 0%

profile of v4, /device:TPU:3, one launch (start us, length us, event | category | flops | bytes accessed | tf_op | source)
XLA Modules:
  0.0 103.1 jit_solution(12821687621612377279)
XLA Ops:
  0.0 1.8 %attention_parts.1 = (f32[4,2,2,16,128]{4,3,2,1,0:T(8,128)S(1)}, bf16[2,2,1536]{2,1,0:T(2,128)(2,1)S(1)}, f32[2,1,1536]{2,1,0:T(1,128)S(1)}) custom-call(s32[2,2]{1,0:T(2,128)} %refs_0_.1, s32[2]{0:T(128)} %refs_1_.2, bf16[2,6144]{1,0:T(2,128)(2,1)} %refs_2_.2, bf16[1,3,64,1024]{3,2,1,0:T(8,128)(2,1)} %refs_3_.1, bf16[1,3,64,1024]{3,2,1,0:T(8,128)(2,1)} %refs_4_.2, ...), custom_call_target="tpu_custom_call" | custom-call | tf_op jit(solution)/shard_map/attention_parts/pallas_call | solution.py:188
  1.8 7.7 %all_to_all.25.parts_ref = f32[4,2,2,16,128]{4,3,2,1,0:T(8,128)S(1)} all-to-all(f32[4,2,2,16,128]{4,3,2,1,0:T(8,128)S(1)} %get-tuple-element.10), channel_id=1, replica_groups=mesh['req'=8,'ctx'=4,'exp'=16] {'ctx'}, dimensions={0} | all-to-all | bytes 262144 | tf_op jit(solution)/shard_map/all_to_all | solution.py:438
  9.6 0.3 merge_parts.1
  9.8 27.1 %all_to_all.26 = bf16[16,2,3200]{2,1,0:T(2,128)(2,1)S(1)} all-to-all(bf16[16,2,3200]{2,1,0:T(2,128)(2,1)S(1)} %get-tuple-element.14), channel_id=1, replica_groups={{0,4,8,12,128,132,136,140,256,260,264,268,384,388,392,396},{2,6,10,14,1..., dimensions={0} | all-to-all | bytes 409600 | tf_op jit(solution)/shard_map/all_to_all | solution.py:442
  36.9 0.1 reshape.16
  37.0 1.3 %broadcast_in_dim.3 = bf16[8,32,3200]{2,1,0:T(8,128)(2,1)} broadcast(bf16[32,3200]{1,0:T(8,128)(2,1)S(1)} %reshape.16), dimensions={1,2} | broadcast | bytes 1843200 | tf_op jit(solution)/shard_map/broadcast_in_dim | solution.py:446
  38.3 6.1 %all-to-all-start.2 = ((bf16[8,32,3200]{2,1,0:T(8,128)(2,1)}), bf16[8,32,3200]{2,1,0:T(8,128)(2,1)S(1)}, u32[]{:S(2)}, u32[]{:S(2)}) async-start(bf16[8,32,3200]{2,1,0:T(8,128)(2,1)} %broadcast_in_dim.3), calls=%async_computation.2 | async-start | bytes 3276800 | tf_op jit(solution)/shard_map/all_to_all | solution.py:442
  44.3 3.9 %collective-permute-start = (bf16[1,96,6144]{2,1,0:T(8,128)(2,1)}, bf16[1,96,6144]{2,1,0:T(8,128)(2,1)S(1)}, u32[]{:S(2)}, u32[]{:S(2)}) collective-permute-start(bf16[1,96,6144]{2,1,0:T(8,128)(2,1)} %refs_2_.3), channel_id=1, source_target_pairs={{0,1},{1,0},{2,3},{3,2},{4,5},{5,4},{6,7},{7,6},{8,9},{9,8},{10,11... | collective-permute-start | bytes 3538952 | tf_op jit(solution)/shard_map/ppermute | solution.py:425
  48.3 1.9 %collective-permute-start.1 = (bf16[1,96,6144]{2,1,0:T(8,128)(2,1)}, bf16[1,96,6144]{2,1,0:T(8,128)(2,1)S(1)}, u32[]{:S(2)}, u32[]{:S(2)}) collective-permute-start(bf16[1,96,6144]{2,1,0:T(8,128)(2,1)} %refs_4_.3), channel_id=1, source_target_pairs={{0,1},{1,0},{2,3},{3,2},{4,5},{5,4},{6,7},{7,6},{8,9},{9,8},{10,11... | collective-permute-start | bytes 3538952 | tf_op jit(solution)/shard_map/ppermute | solution.py:425
  50.2 2.4 %collective-permute-start.2 = (bf16[1,96,6144]{2,1,0:T(8,128)(2,1)}, bf16[1,96,6144]{2,1,0:T(8,128)(2,1)S(1)}, u32[]{:S(2)}, u32[]{:S(2)}) collective-permute-start(bf16[1,96,6144]{2,1,0:T(8,128)(2,1)} %refs_1_.3), channel_id=1, source_target_pairs={{0,1},{1,0},{2,3},{3,2},{4,5},{5,4},{6,7},{7,6},{8,9},{9,8},{10,11... | collective-permute-start | bytes 3538952 | tf_op jit(solution)/shard_map/ppermute | solution.py:425
  52.6 0.0 collective-permute-done.refs_0_
  52.6 0.0 copy-start
  52.6 0.6 collective-permute-done.1.refs_3_
  53.2 0.4 copy-done
  53.7 0.0 copy-start.1
  53.7 1.0 copy-done.1
  54.7 0.6 collective-permute-done.2.refs_5_
  55.3 0.2 all-to-all-done.2
  55.5 3.7 %expert_partials.1 = bf16[2,4,2,32,1536]{4,3,2,1,0:T(8,128)(2,1)S(1)} custom-call(s32[16]{0:T(128)} %block_source.1, s32[16,4,16]{2,1,0:T(4,128)} %bitcast.7, f32[16,4,16]{2,1,0:T(4,128)} %bitcast.8, bf16[2,4,32,3200]{3,2,1,0:T(8,128)(2,1)S(1)} %bitcast.5, bf16[1,96,6144]{2,1,0:T(8,128)(2,1)} %copy-done, bf16[1,96,6144]{2,1,0:T(8,128)(2,1)} %refs_1_.3, ...), custom_call_target="tpu_custom_call" | custom-call | flops 905969664 | bytes 7077888 | tf_op jit(solution)/shard_map/expert_partials/pallas_call | solution.py:372
  59.1 17.7 %all_to_all.27 = bf16[8,2,32,1536]{3,2,1,0:T(8,128)(2,1)S(1)} all-to-all(bf16[8,2,32,1536]{3,2,1,0:T(8,128)(2,1)S(1)} %bitcast.6), channel_id=1, replica_groups={{0,2,64,66,16,18,80,82},{4,6,68,70,20,22,84,86},{8,10,72,74,24,26,88,90..., dimensions={0} | all-to-all | bytes 3145728 | tf_op jit(solution)/shard_map/all_to_all | solution.py:442
  76.9 0.2 reduce_sum.21
  77.1 0.1 reshape.19
  77.2 25.3 %all_to_all.28 = bf16[32,2,1536]{2,1,0:T(2,128)(2,1)S(1)} all-to-all(bf16[32,2,1536]{2,1,0:T(2,128)(2,1)S(1)} %reshape.19), channel_id=1, replica_groups={{0,4,8,12,128,132,136,140,256,260,264,268,384,388,392,396,32,36,40,44,1..., dimensions={0} | all-to-all | bytes 393216 | tf_op jit(solution)/shard_map/all_to_all | solution.py:442
  102.5 0.6 add_convert_fusion
  (1 shorter events, 0.0 us)
Async XLA Ops:
  38.3 17.2 %all-to-all-start.2 = ((bf16[8,32,3200]{2,1,0:T(8,128)(2,1)}), bf16[8,32,3200]{2,1,0:T(8,128)(2,1)S(1)}, u32[]{:S(2)}, u32[]{:S(2)}) async-start(bf16[8,32,3200]{2,1,0:T(8,128)(2,1)} %broadcast_in_dim.3), calls=%async_computation.2 | async-start | bytes 3276800 | tf_op jit(solution)/shard_map/all_to_all | solution.py:442
  44.3 8.3 %collective-permute-start = (bf16[1,96,6144]{2,1,0:T(8,128)(2,1)}, bf16[1,96,6144]{2,1,0:T(8,128)(2,1)S(1)}, u32[]{:S(2)}, u32[]{:S(2)}) collective-permute-start(bf16[1,96,6144]{2,1,0:T(8,128)(2,1)} %refs_2_.3), channel_id=1, source_target_pairs={{0,1},{1,0},{2,3},{3,2},{4,5},{5,4},{6,7},{7,6},{8,9},{9,8},{10,11... | collective-permute-start | bytes 3538952 | tf_op jit(solution)/shard_map/ppermute | solution.py:425
  48.3 5.0 %collective-permute-start.1 = (bf16[1,96,6144]{2,1,0:T(8,128)(2,1)}, bf16[1,96,6144]{2,1,0:T(8,128)(2,1)S(1)}, u32[]{:S(2)}, u32[]{:S(2)}) collective-permute-start(bf16[1,96,6144]{2,1,0:T(8,128)(2,1)} %refs_4_.3), channel_id=1, source_target_pairs={{0,1},{1,0},{2,3},{3,2},{4,5},{5,4},{6,7},{7,6},{8,9},{9,8},{10,11... | collective-permute-start | bytes 3538952 | tf_op jit(solution)/shard_map/ppermute | solution.py:425
  50.2 5.1 %collective-permute-start.2 = (bf16[1,96,6144]{2,1,0:T(8,128)(2,1)}, bf16[1,96,6144]{2,1,0:T(8,128)(2,1)S(1)}, u32[]{:S(2)}, u32[]{:S(2)}) collective-permute-start(bf16[1,96,6144]{2,1,0:T(8,128)(2,1)} %refs_1_.3), channel_id=1, source_target_pairs={{0,1},{1,0},{2,3},{3,2},{4,5},{5,4},{6,7},{7,6},{8,9},{9,8},{10,11... | collective-permute-start | bytes 3538952 | tf_op jit(solution)/shard_map/ppermute | solution.py:425
  52.6 1.0 copy-start
  53.7 1.0 copy-start.1

commit v5 on v4

--- a/solution.py
+++ b/solution.py
@@ -18,6 +18,7 @@
 LANES = 128
 KERNEL_VMEM = 16 << 20
 AXES = ("req", "ctx", "exp")
+QUARTERS = ((0, 0), (1, 0), (1, 1), (0, 1))
 F32 = jnp.float32
 BF16 = jnp.bfloat16
 
@@ -40,9 +41,8 @@
     near = [
         [
             device(2 * zh + zl, 2 * xh + xl, 2 * yh + yl, core)
-            for xl in (0, 1)
-            for zl in (0, 1)
-            for yl in (0, 1)
+            for quarter, (zl, yl) in enumerate(QUARTERS)
+            for xl in (quarter % 2, 1 - quarter % 2)
         ]
         for core in (0, 1)
         for xh in range(n_ctx // 2)
@@ -52,9 +52,9 @@
     far = [
         [
             device(2 * zh + zl, 2 * xh + xl, 2 * yh + yl, core)
+            for yh in range(cols // 2)
+            for zh in range(n_req // 2)
             for xh in range(n_ctx // 2)
-            for zh in range(n_req // 2)
-            for yh in range(cols // 2)
         ]
         for core in (0, 1)
         for xl in (0, 1)
@@ -278,7 +278,8 @@
     request, row = row % requests, row // requests
     yh, row = row % half_y, row // half_y
     zh, row = row % (n_req // 2), row // (n_req // 2)
-    yl, zl = row % 2, row // 2
+    zl = sum((row == q).astype(jnp.int32) * QUARTERS[q][0] for q in range(4))
+    yl = sum((row == q).astype(jnp.int32) * QUARTERS[q][1] for q in range(4))
     here = entry == (2 * zh + zl + core) % n_req * requests + request
     y = (2 * yh + yl + core) % (n_exp // 2)
     diagonal = lax.broadcasted_iota(jnp.int32, (entries, entries), 0) == lax.broadcasted_iota(
@@ -307,7 +308,7 @@
     for copy in copies[:3]:
         copy.wait()
     copies = copies[3:]
-    n_xl, quarters, n_xh, far_rows, width = out_ref.shape
+    quarters, n_xl, n_xh, far_rows, width = out_ref.shape
     n_ctx, rows, hidden = n_xl * n_xh, quarters * far_rows, held[0].shape[1]
     contract = (((1,), (1,)), ((), ()))
     ones = jnp.ones((8, LANES), BF16)
@@ -321,17 +322,22 @@
         column = lax.rem(chunk + n_ctx - core, n_ctx)
         return column % n_xl, column // n_xl
 
+    def own_rows(xl, columns):
+        return jnp.concatenate(
+            [tokens_ref[q, (xl + q) % n_xl, :, columns] for q in range(quarters)], axis=0
+        )
+
     def added(total, term):
         return term if total is None else total + term
 
     squares = None
     for xl in range(n_xl):
-        tokens = tokens_ref[xl, :, :, n_xh * width :].reshape(rows, LANES)
+        tokens = own_rows(xl, slice(n_xh * width, n_xh * width + LANES))
         squares = added(
             squares, lax.dot_general(ones, tokens, contract, preferred_element_type=F32)
         )
         for xh in range(n_xh):
-            tokens = tokens_ref[xl, :, :, xh * width : (xh + 1) * width].reshape(rows, width)
+            tokens = own_rows(xl, slice(xh * width, (xh + 1) * width))
             turned[lax.rem(xh * n_xl + xl + core, n_ctx)] = tokens.T
     scale = lax.rsqrt(squares[:1] / model_width + EPSILON)
     active = []
@@ -356,13 +362,14 @@
         columns = slice(chunk * width, (chunk + 1) * width)
         down = jnp.concatenate([w[0, :, columns] for w in held[4:]], axis=0)
         total = jnp.dot(active, down, preferred_element_type=F32).astype(BF16)
-        out_ref[xl, :, xh] = total.reshape(quarters, far_rows, width)
+        for q in range(quarters):
+            out_ref[q, lax.rem(xl + q, n_xl), xh] = total[q * far_rows : (q + 1) * far_rows]
 
 
 def expert_partials(
     tokens, routes, route_weights, block_expert, gate_other, weights, requests
 ):
-    n_xl, quarters, far_rows, padded = tokens.shape
+    quarters, n_xl, far_rows, padded = tokens.shape
     n_xh = 2
     width = (padded - LANES) // n_xh
     rows, model_width = quarters * far_rows, width * n_xl * n_xh
@@ -371,7 +378,7 @@
     vmem = pl.BlockSpec(memory_space=pltpu.VMEM)
     return pl.pallas_call(
         functools.partial(expert_kernel, float(model_width), requests),
-        out_shape=pltpu.VMEM((n_xl, quarters, n_xh, far_rows, width), BF16),
+        out_shape=pltpu.VMEM((quarters, n_xl, n_xh, far_rows, width), BF16),
         in_specs=[hbm, hbm, hbm, vmem] + [hbm] * len(weights) + [vmem],
         out_specs=vmem,
         scratch_shapes=[pltpu.VMEM(w.shape, w.dtype) for w in weights]
@@ -444,7 +451,7 @@
     tokens = exchange(piece, columns_far)
     tokens = tokens.reshape(far_rows, piece.shape[2])
     tokens = exchange(jnp.broadcast_to(tokens, (n_near,) + tokens.shape), near)
-    tokens = tokens.reshape(2, n_near // 2, far_rows, piece.shape[2])
+    tokens = tokens.reshape(n_near // 2, 2, far_rows, piece.shape[2])
     partials = expert_partials(
         tokens,
         expert_routes.transpose(0, 2, 1),
@@ -456,7 +463,9 @@
     )
     partials = exchange(partials.reshape(n_near, 2, far_rows, width), near)
     partials = jnp.sum(partials.astype(F32), axis=0).astype(BF16)
-    partials = exchange(partials.reshape(n_far, requests, width), far)
+    partials = partials.reshape(2, n_req // 2, n_exp // 4, requests, width)
+    partials = partials.transpose(2, 1, 0, 3, 4).reshape(n_far, requests, width)
+    partials = exchange(partials, far)
     expert_sum = jnp.sum(partials.astype(F32), axis=0)
     return (stream.astype(F32) + expert_sum).astype(BF16)
 

time: 104 us -> 103 us (level)
  the two profiles are of different devices: /device:TPU:3 before, /device:TPU:9 now
where the time goes in v5:
time: 103 us; the launch traced here: 102 us
  blocking collectives  74.7 us (73%)
  starting transfers between devices  12.9 us (13%)
  Pallas kernels  5.8 us (6%)
  waiting for transfers between devices  4.94 us (5%)
  local copies, waits for them, and re-layouts  3.04 us (3%)
    all_to_all x3, blocking collectives, exchange(): return lax.all_to_all(x, AXES, 0, 0, axis_index_groups=groups, tiled=True)  66 us
    all_to_all x1, blocking collectives, on_device(): parts = lax.all_to_all(parts, 'ctx', 0, 0, tiled=True)  8.64 us
    all_to_all x1, starting transfers between devices, exchange(): return lax.all_to_all(x, AXES, 0, 0, axis_index_groups=groups, tiled=True)  6.66 us
    ppermute x3, starting transfers between devices, on_device(): lax.ppermute(w, 'exp', swap)  6.24 us
    pallas_call x1, Pallas kernels, expert_partials(): pl.pallas_call(functools.partial(expert_kernel, float(model_width), reque...  3.69 us
    all_to_all x1, waiting for transfers between devices, exchange(): return lax.all_to_all(x, AXES, 0, 0, axis_index_groups=groups, tiled=True)  3.26 us
  transfers between devices with their start and end apart: 4, of which 3 were waited for; matrix products, arithmetic and copies ran while one was open for 0% of the time, Pallas kernels for 0%

profile of v5, /device:TPU:9, one launch (start us, length us, event | category | flops | bytes accessed | tf_op | source)
XLA Modules:
  0.0 102.4 jit_solution(5206829785298871862)
XLA Ops:
  0.0 1.8 %attention_parts.1 = (f32[4,2,2,16,128]{4,3,2,1,0:T(8,128)S(1)}, bf16[2,2,1536]{2,1,0:T(2,128)(2,1)S(1)}, f32[2,1,1536]{2,1,0:T(1,128)S(1)}) custom-call(s32[2,2]{1,0:T(2,128)} %refs_0_.1, s32[2]{0:T(128)} %refs_1_.2, bf16[2,6144]{1,0:T(2,128)(2,1)} %refs_2_.2, bf16[1,3,64,1024]{3,2,1,0:T(8,128)(2,1)} %refs_3_.1, bf16[1,3,64,1024]{3,2,1,0:T(8,128)(2,1)} %refs_4_.2, ...), custom_call_target="tpu_custom_call" | custom-call | tf_op jit(solution)/shard_map/attention_parts/pallas_call | solution.py:188
  1.8 8.6 %all_to_all.25.parts_ref = f32[4,2,2,16,128]{4,3,2,1,0:T(8,128)S(1)} all-to-all(f32[4,2,2,16,128]{4,3,2,1,0:T(8,128)S(1)} %get-tuple-element.10), channel_id=1, replica_groups=mesh['req'=8,'ctx'=4,'exp'=16] {'ctx'}, dimensions={0} | all-to-all | bytes 262144 | tf_op jit(solution)/shard_map/all_to_all | solution.py:445
  10.5 0.3 merge_parts.1
  10.8 29.0 %all_to_all.26 = bf16[16,2,3200]{2,1,0:T(2,128)(2,1)S(1)} all-to-all(bf16[16,2,3200]{2,1,0:T(2,128)(2,1)S(1)} %get-tuple-element.14), channel_id=1, replica_groups={{0,4,8,12,128,132,136,140,256,260,264,268,384,388,392,396},{2,6,10,14,1..., dimensions={0} | all-to-all | bytes 409600 | tf_op jit(solution)/shard_map/all_to_all | solution.py:449
  39.8 0.1 reshape.19
  39.9 1.3 %broadcast_in_dim.3 = bf16[8,32,3200]{2,1,0:T(8,128)(2,1)} broadcast(bf16[32,3200]{1,0:T(8,128)(2,1)S(1)} %reshape.19), dimensions={1,2} | broadcast | bytes 1843200 | tf_op jit(solution)/shard_map/broadcast_in_dim | solution.py:453
  41.1 6.7 %all-to-all-start.2 = ((bf16[8,32,3200]{2,1,0:T(8,128)(2,1)}), bf16[8,32,3200]{2,1,0:T(8,128)(2,1)S(1)}, u32[]{:S(2)}, u32[]{:S(2)}) async-start(bf16[8,32,3200]{2,1,0:T(8,128)(2,1)} %broadcast_in_dim.3), calls=%async_computation.2 | async-start | bytes 3276800 | tf_op jit(solution)/shard_map/all_to_all | solution.py:449
  47.8 1.9 %collective-permute-start = (bf16[1,96,6144]{2,1,0:T(8,128)(2,1)}, bf16[1,96,6144]{2,1,0:T(8,128)(2,1)S(1)}, u32[]{:S(2)}, u32[]{:S(2)}) collective-permute-start(bf16[1,96,6144]{2,1,0:T(8,128)(2,1)} %refs_2_.3), channel_id=1, source_target_pairs={{0,1},{1,0},{2,3},{3,2},{4,5},{5,4},{6,7},{7,6},{8,9},{9,8},{10,11... | collective-permute-start | bytes 3538952 | tf_op jit(solution)/shard_map/ppermute | solution.py:432
  49.7 2.4 %collective-permute-start.1 = (bf16[1,96,6144]{2,1,0:T(8,128)(2,1)}, bf16[1,96,6144]{2,1,0:T(8,128)(2,1)S(1)}, u32[]{:S(2)}, u32[]{:S(2)}) collective-permute-start(bf16[1,96,6144]{2,1,0:T(8,128)(2,1)} %refs_4_.3), channel_id=1, source_target_pairs={{0,1},{1,0},{2,3},{3,2},{4,5},{5,4},{6,7},{7,6},{8,9},{9,8},{10,11... | collective-permute-start | bytes 3538952 | tf_op jit(solution)/shard_map/ppermute | solution.py:432
  52.1 1.9 %collective-permute-start.2 = (bf16[1,96,6144]{2,1,0:T(8,128)(2,1)}, bf16[1,96,6144]{2,1,0:T(8,128)(2,1)S(1)}, u32[]{:S(2)}, u32[]{:S(2)}) collective-permute-start(bf16[1,96,6144]{2,1,0:T(8,128)(2,1)} %refs_1_.3), channel_id=1, source_target_pairs={{0,1},{1,0},{2,3},{3,2},{4,5},{5,4},{6,7},{7,6},{8,9},{9,8},{10,11... | collective-permute-start | bytes 3538952 | tf_op jit(solution)/shard_map/ppermute | solution.py:432
  54.1 0.0 collective-permute-done.refs_0_
  54.1 0.0 copy-start
  54.1 0.7 collective-permute-done.1.refs_3_
  54.8 0.3 copy-done
  55.1 0.0 copy-start.1
  55.1 1.0 copy-done.1
  56.1 1.0 collective-permute-done.2.refs_5_
  57.1 3.3 %all-to-all-done.2 = bf16[8,32,3200]{2,1,0:T(8,128)(2,1)S(1)} async-done(((bf16[8,32,3200]{2,1,0:T(8,128)(2,1)}), bf16[8,32,3200]{2,1,0:T(8,128)(2,1)S(1)}, u32[]{:S(2)}, u32[]{:S(2)}) %all-to-all-start.2) | async-done | bytes 1638432 | tf_op jit(solution)/shard_map/all_to_all | solution.py:449
  60.3 3.7 %expert_partials.1 = bf16[4,2,2,32,1536]{4,3,2,1,0:T(8,128)(2,1)S(1)} custom-call(s32[16]{0:T(128)} %block_source.1, s32[16,4,16]{2,1,0:T(4,128)} %bitcast.13, f32[16,4,16]{2,1,0:T(4,128)} %bitcast.14, bf16[4,2,32,3200]{3,2,1,0:T(8,128)(2,1)S(1)} %bitcast.9, bf16[1,96,6144]{2,1,0:T(8,128)(2,1)} %copy-done, bf16[1,96,6144]{2,1,0:T(8,128)(2,1)} %refs_1_.3, ...), custom_call_target="tpu_custom_call" | custom-call | flops 905969664 | bytes 7077888 | tf_op jit(solution)/shard_map/expert_partials/pallas_call | solution.py:379
  64.0 16.8 %all_to_all.27 = bf16[8,2,32,1536]{3,2,1,0:T(8,128)(2,1)S(1)} all-to-all(bf16[8,2,32,1536]{3,2,1,0:T(8,128)(2,1)S(1)} %bitcast.10), channel_id=1, replica_groups={{0,16,80,64,66,82,18,2},{4,20,84,68,70,86,22,6},{8,24,88,72,74,90,26,10..., dimensions={0} | all-to-all | bytes 3145728 | tf_op jit(solution)/shard_map/all_to_all | solution.py:449
  80.9 0.2 reduce_sum.21
  81.1 0.2 copy.15
  81.3 0.2 copy.16
  81.5 20.2 %all_to_all.28 = bf16[32,2,1536]{2,1,0:T(2,128)(2,1)S(1)} all-to-all(bf16[32,2,1536]{2,1,0:T(2,128)(2,1)S(1)} %bitcast.12), channel_id=1, replica_groups={{0,32,128,160,256,288,384,416,4,36,132,164,260,292,388,420,8,40,136,168..., dimensions={0} | all-to-all | bytes 393216 | tf_op jit(solution)/shard_map/all_to_all | solution.py:449
  101.7 0.2 convert_reduce_fusion
  101.8 0.6 add_convert_fusion
Async XLA Ops:
  41.1 19.2 %all-to-all-start.2 = ((bf16[8,32,3200]{2,1,0:T(8,128)(2,1)}), bf16[8,32,3200]{2,1,0:T(8,128)(2,1)S(1)}, u32[]{:S(2)}, u32[]{:S(2)}) async-start(bf16[8,32,3200]{2,1,0:T(8,128)(2,1)} %broadcast_in_dim.3), calls=%async_computation.2 | async-start | bytes 3276800 | tf_op jit(solution)/shard_map/all_to_all | solution.py:449
  47.8 6.3 %collective-permute-start = (bf16[1,96,6144]{2,1,0:T(8,128)(2,1)}, bf16[1,96,6144]{2,1,0:T(8,128)(2,1)S(1)}, u32[]{:S(2)}, u32[]{:S(2)}) collective-permute-start(bf16[1,96,6144]{2,1,0:T(8,128)(2,1)} %refs_2_.3), channel_id=1, source_target_pairs={{0,1},{1,0},{2,3},{3,2},{4,5},{5,4},{6,7},{7,6},{8,9},{9,8},{10,11... | collective-permute-start | bytes 3538952 | tf_op jit(solution)/shard_map/ppermute | solution.py:432
  49.7 5.1 %collective-permute-start.1 = (bf16[1,96,6144]{2,1,0:T(8,128)(2,1)}, bf16[1,96,6144]{2,1,0:T(8,128)(2,1)S(1)}, u32[]{:S(2)}, u32[]{:S(2)}) collective-permute-start(bf16[1,96,6144]{2,1,0:T(8,128)(2,1)} %refs_4_.3), channel_id=1, source_target_pairs={{0,1},{1,0},{2,3},{3,2},{4,5},{5,4},{6,7},{7,6},{8,9},{9,8},{10,11... | collective-permute-start | bytes 3538952 | tf_op jit(solution)/shard_map/ppermute | solution.py:432
  52.1 5.0 %collective-permute-start.2 = (bf16[1,96,6144]{2,1,0:T(8,128)(2,1)}, bf16[1,96,6144]{2,1,0:T(8,128)(2,1)S(1)}, u32[]{:S(2)}, u32[]{:S(2)}) collective-permute-start(bf16[1,96,6144]{2,1,0:T(8,128)(2,1)} %refs_1_.3), channel_id=1, source_target_pairs={{0,1},{1,0},{2,3},{3,2},{4,5},{5,4},{6,7},{7,6},{8,9},{9,8},{10,11... | collective-permute-start | bytes 3538952 | tf_op jit(solution)/shard_map/ppermute | solution.py:432
  54.1 1.0 %copy-start = (bf16[1,96,6144]{2,1,0:T(8,128)(2,1)}, bf16[1,96,6144]{2,1,0:T(8,128)(2,1)S(1)}, u32[]{:S(2)}) copy-start(bf16[1,96,6144]{2,1,0:T(8,128)(2,1)S(1)} %collective-permute-done.refs_0_) | copy-start | bytes 3538948
  55.1 1.0 copy-start.1

commit v6 on v5

--- a/solution.py
+++ b/solution.py
@@ -75,6 +75,18 @@
     return near, far, columns_far
 
 
+def terms(x):
+    first = x.astype(BF16).astype(F32)
+    second = (x - first).astype(BF16).astype(F32)
+    return [first, second, x - first - second]
+
+
+def statistic_lanes():
+    row = lax.broadcasted_iota(jnp.int32, (ROWS, LANES), 0)
+    lane = lax.broadcasted_iota(jnp.int32, (ROWS, LANES), 1)
+    return [lane == row + term * ROWS for term in range(6)]
+
+
 def started(sources, targets, arrived):
     copies = [
         pltpu.make_async_copy(source, target, arrived.at[i])
@@ -120,7 +132,7 @@
             seen = here if seen is None else seen | here
         live = seen if live is None else jnp.where(row_id < r * GROUP, live.astype(jnp.int32), seen.astype(jnp.int32)) > 0
     out_row = lax.broadcasted_iota(jnp.int32, (ROWS, LANES), 0)
-    diagonal = out_row == lax.broadcasted_iota(jnp.int32, (ROWS, LANES), 1)
+    places = statistic_lanes()
     live = jnp.concatenate([live] * KV_HEADS, axis=0)
     copies[3].wait()
     keys = k_ref[0].reshape(positions, KV_HEADS * HEAD_DIM)
@@ -160,11 +172,11 @@
             preferred_element_type=F32,
         )
         mixes = mixes[:ROWS] + mixes[ROWS:]
-        top_row = jnp.sum(jnp.where(diagonal, top[rows(k)], 0.0), axis=0, keepdims=True)
-        total_row = jnp.sum(jnp.where(diagonal, total[rows(k)], 0.0), axis=0, keepdims=True)
-        part = jnp.where(
-            out_row < used, mixes, jnp.where(out_row == used, top_row, total_row)
-        )
+        statistics = 0.0
+        for here, term in zip(places, terms(top[rows(k)]) + terms(total[rows(k)])):
+            statistics = jnp.where(here, term, statistics)
+        statistics = jnp.sum(statistics, axis=0, keepdims=True)
+        part = jnp.where(out_row < used, mixes, statistics).astype(BF16)
         chunk, k = divmod(k, KV_HEADS // n_ctx)
         out_ref[chunk, 0, k] = part
         out_ref[(chunk + n_ctx // 2) % n_ctx, 1, k] = part
@@ -188,7 +200,7 @@
     return pl.pallas_call(
         functools.partial(attention_kernel, n_ctx),
         out_shape=(
-            pltpu.VMEM((n_ctx, 2, KV_HEADS // n_ctx, ROWS, HEAD_DIM), F32),
+            pltpu.VMEM((n_ctx, 2, KV_HEADS // n_ctx, ROWS, HEAD_DIM), BF16),
             pltpu.VMEM((2, residual.shape[0], residual.shape[1] // n_ctx), BF16),
             pltpu.VMEM((2, 1, residual.shape[1] // n_ctx), F32),
         ),
@@ -209,21 +221,23 @@
     used = requests * GROUP
     place = lax.axis_index("ctx")
     core = lax.rem(lax.axis_index("exp"), 2)
-    diagonal = lax.broadcasted_iota(jnp.int32, (ROWS, LANES), 0) == lax.broadcasted_iota(
-        jnp.int32, (ROWS, LANES), 1
-    )
-
-    def column(row):
-        return jnp.sum(jnp.where(diagonal, row, 0.0), axis=1, keepdims=True)
+    places = statistic_lanes()
+    top_lanes = places[0] | places[1] | places[2]
+    total_lanes = places[3] | places[4] | places[5]
+
+    def column(part, lanes):
+        row = part[used : used + 1, :]
+        return jnp.sum(jnp.where(lanes, row, 0.0), axis=1, keepdims=True)
 
     scaled, square = [], 0.0
     for i in range(2):
         for k in range(kv_here):
-            tops = [column(parts_ref[s, i, k, used : used + 1, :]) for s in range(n_src)]
-            totals = [column(parts_ref[s, i, k, used + 1 : used + 2, :]) for s in range(n_src)]
+            parts = [parts_ref[s, i, k].astype(F32) for s in range(n_src)]
+            tops = [column(part, top_lanes) for part in parts]
+            totals = [column(part, total_lanes) for part in parts]
             top = functools.reduce(jnp.maximum, tops)
             scales = [jnp.exp(t - top) for t in tops]
-            mixes = sum(parts_ref[s, i, k] * scales[s] for s in range(n_src))
+            mixes = sum(parts[s] * scales[s] for s in range(n_src))
             total = sum(totals[s] * scales[s] for s in range(n_src))
             mixes = mixes / total
             for r in range(requests):
@@ -237,9 +251,7 @@
         wide = stream.astype(F32)
         scaled.append(wide * gain_ref[i])
         square += jnp.sum(wide * wide, axis=1, keepdims=True)
-    first = square.astype(BF16).astype(F32)
-    second = (square - first).astype(BF16).astype(F32)
-    third = square - first - second
+    first, second, third = terms(square)
     lane = lax.broadcasted_iota(jnp.int32, (requests, LANES), 1)
     spread = jnp.where(
         lane == 0, first, jnp.where(lane == 1, second, jnp.where(lane == 2, third, 0.0))

time: 103 us -> 103 us (level)
  the two profiles are of different devices: /device:TPU:9 before, /device:TPU:65 now
where the time goes in v6:
time: 103 us; the launch traced here: 102 us
  blocking collectives  74.4 us (72%)
  starting transfers between devices  14.2 us (14%)
  Pallas kernels  5.81 us (6%)
  waiting for transfers between devices  3.58 us (3%)
  local copies, waits for them, and re-layouts  3.04 us (3%)
    all_to_all x3, blocking collectives, exchange(): return lax.all_to_all(x, AXES, 0, 0, axis_index_groups=groups, tiled=True)  66.1 us
    all_to_all x1, blocking collectives, on_device(): parts = lax.all_to_all(parts, 'ctx', 0, 0, tiled=True)  8.29 us
    all_to_all x1, starting transfers between devices, exchange(): return lax.all_to_all(x, AXES, 0, 0, axis_index_groups=groups, tiled=True)  7.94 us
    ppermute x3, starting transfers between devices, on_device(): lax.ppermute(w, 'exp', swap)  6.24 us
    pallas_call x1, Pallas kernels, expert_partials(): pl.pallas_call(functools.partial(expert_kernel, float(model_width), reque...  3.7 us
  transfers between devices with their start and end apart: 4, of which 3 were waited for; matrix products, arithmetic and copies ran while one was open for 0% of the time, Pallas kernels for 0%

profile of v6, /device:TPU:65, one launch (start us, length us, event | category | flops | bytes accessed | tf_op | source)
XLA Modules:
  0.0 102.1 jit_solution(1117587670156822606)
XLA Ops:
  0.0 1.8 %attention_parts.1 = (bf16[4,2,2,16,128]{4,3,2,1,0:T(8,128)(2,1)S(1)}, bf16[2,2,1536]{2,1,0:T(2,128)(2,1)S(1)}, f32[2,1,1536]{2,1,0:T(1,128)S(1)}) custom-call(s32[2,2]{1,0:T(2,128)} %refs_0_.1, s32[2]{0:T(128)} %refs_1_.2, bf16[2,6144]{1,0:T(2,128)(2,1)} %refs_2_.2, bf16[1,3,64,1024]{3,2,1,0:T(8,128)(2,1)} %refs_3_.1, bf16[1,3,64,1024]{3,2,1,0:T(8,128)(2,1)} %refs_4_.2, ...), custom_call_target="tpu_custom_call" | custom-call | tf_op jit(solution)/shard_map/attention_parts/pallas_call | solution.py:200
  1.8 8.3 %all_to_all.25.parts_ref = bf16[4,2,2,16,128]{4,3,2,1,0:T(8,128)(2,1)S(1)} all-to-all(bf16[4,2,2,16,128]{4,3,2,1,0:T(8,128)(2,1)S(1)} %get-tuple-element.10), channel_id=1, replica_groups=mesh['req'=8,'ctx'=4,'exp'=16] {'ctx'}, dimensions={0} | all-to-all | bytes 131072 | tf_op jit(solution)/shard_map/all_to_all | solution.py:457
  10.1 0.3 merge_parts.1
  10.4 26.0 %all_to_all.26 = bf16[16,2,3200]{2,1,0:T(2,128)(2,1)S(1)} all-to-all(bf16[16,2,3200]{2,1,0:T(2,128)(2,1)S(1)} %get-tuple-element.14), channel_id=1, replica_groups={{0,4,8,12,128,132,136,140,256,260,264,268,384,388,392,396},{2,6,10,14,1..., dimensions={0} | all-to-all | bytes 409600 | tf_op jit(solution)/shard_map/all_to_all | solution.py:461
  36.4 0.1 reshape.19
  36.5 1.3 %broadcast_in_dim.3 = bf16[8,32,3200]{2,1,0:T(8,128)(2,1)} broadcast(bf16[32,3200]{1,0:T(8,128)(2,1)S(1)} %reshape.19), dimensions={1,2} | broadcast | bytes 1843200 | tf_op jit(solution)/shard_map/broadcast_in_dim | solution.py:465
  37.7 7.9 %all-to-all-start.2 = ((bf16[8,32,3200]{2,1,0:T(8,128)(2,1)}), bf16[8,32,3200]{2,1,0:T(8,128)(2,1)S(1)}, u32[]{:S(2)}, u32[]{:S(2)}) async-start(bf16[8,32,3200]{2,1,0:T(8,128)(2,1)} %broadcast_in_dim.3), calls=%async_computation.2 | async-start | bytes 3276800 | tf_op jit(solution)/shard_map/all_to_all | solution.py:461
  45.7 1.9 %collective-permute-start = (bf16[1,96,6144]{2,1,0:T(8,128)(2,1)}, bf16[1,96,6144]{2,1,0:T(8,128)(2,1)S(1)}, u32[]{:S(2)}, u32[]{:S(2)}) collective-permute-start(bf16[1,96,6144]{2,1,0:T(8,128)(2,1)} %refs_2_.3), channel_id=1, source_target_pairs={{0,1},{1,0},{2,3},{3,2},{4,5},{5,4},{6,7},{7,6},{8,9},{9,8},{10,11... | collective-permute-start | bytes 3538952 | tf_op jit(solution)/shard_map/ppermute | solution.py:444
  47.6 2.4 %collective-permute-start.1 = (bf16[1,96,6144]{2,1,0:T(8,128)(2,1)}, bf16[1,96,6144]{2,1,0:T(8,128)(2,1)S(1)}, u32[]{:S(2)}, u32[]{:S(2)}) collective-permute-start(bf16[1,96,6144]{2,1,0:T(8,128)(2,1)} %refs_4_.3), channel_id=1, source_target_pairs={{0,1},{1,0},{2,3},{3,2},{4,5},{5,4},{6,7},{7,6},{8,9},{9,8},{10,11... | collective-permute-start | bytes 3538952 | tf_op jit(solution)/shard_map/ppermute | solution.py:444
  50.0 1.9 %collective-permute-start.2 = (bf16[1,96,6144]{2,1,0:T(8,128)(2,1)}, bf16[1,96,6144]{2,1,0:T(8,128)(2,1)S(1)}, u32[]{:S(2)}, u32[]{:S(2)}) collective-permute-start(bf16[1,96,6144]{2,1,0:T(8,128)(2,1)} %refs_1_.3), channel_id=1, source_target_pairs={{0,1},{1,0},{2,3},{3,2},{4,5},{5,4},{6,7},{7,6},{8,9},{9,8},{10,11... | collective-permute-start | bytes 3538952 | tf_op jit(solution)/shard_map/ppermute | solution.py:444
  51.9 0.0 collective-permute-done.refs_0_
  52.0 0.0 copy-start
  52.0 0.7 collective-permute-done.1.refs_3_
  52.7 0.3 copy-done
  53.0 0.0 copy-start.1
  53.0 1.0 copy-done.1
  54.0 1.0 collective-permute-done.2.refs_5_
  55.0 1.9 %all-to-all-done.2 = bf16[8,32,3200]{2,1,0:T(8,128)(2,1)S(1)} async-done(((bf16[8,32,3200]{2,1,0:T(8,128)(2,1)}), bf16[8,32,3200]{2,1,0:T(8,128)(2,1)S(1)}, u32[]{:S(2)}, u32[]{:S(2)}) %all-to-all-start.2) | async-done | bytes 1638432 | tf_op jit(solution)/shard_map/all_to_all | solution.py:461
  56.9 3.7 %expert_partials.1 = bf16[4,2,2,32,1536]{4,3,2,1,0:T(8,128)(2,1)S(1)} custom-call(s32[16]{0:T(128)} %block_source.1, s32[16,4,16]{2,1,0:T(4,128)} %bitcast.13, f32[16,4,16]{2,1,0:T(4,128)} %bitcast.14, bf16[4,2,32,3200]{3,2,1,0:T(8,128)(2,1)S(1)} %bitcast.9, bf16[1,96,6144]{2,1,0:T(8,128)(2,1)} %copy-done, bf16[1,96,6144]{2,1,0:T(8,128)(2,1)} %refs_1_.3, ...), custom_call_target="tpu_custom_call" | custom-call | flops 905969664 | bytes 7077888 | tf_op jit(solution)/shard_map/expert_partials/pallas_call | solution.py:391
  60.6 16.8 %all_to_all.27 = bf16[8,2,32,1536]{3,2,1,0:T(8,128)(2,1)S(1)} all-to-all(bf16[8,2,32,1536]{3,2,1,0:T(8,128)(2,1)S(1)} %bitcast.10), channel_id=1, replica_groups={{0,16,80,64,66,82,18,2},{4,20,84,68,70,86,22,6},{8,24,88,72,74,90,26,10..., dimensions={0} | all-to-all | bytes 3145728 | tf_op jit(solution)/shard_map/all_to_all | solution.py:461
  77.4 0.2 reduce_sum.21
  77.6 0.2 copy.15
  77.8 0.2 copy.16
  78.0 23.4 %all_to_all.28 = bf16[32,2,1536]{2,1,0:T(2,128)(2,1)S(1)} all-to-all(bf16[32,2,1536]{2,1,0:T(2,128)(2,1)S(1)} %bitcast.12), channel_id=1, replica_groups={{0,32,128,160,256,288,384,416,4,36,132,164,260,292,388,420,8,40,136,168..., dimensions={0} | all-to-all | bytes 393216 | tf_op jit(solution)/shard_map/all_to_all | solution.py:461
  101.4 0.2 convert_reduce_fusion
  101.5 0.6 add_convert_fusion
Async XLA Ops:
  37.7 19.1 %all-to-all-start.2 = ((bf16[8,32,3200]{2,1,0:T(8,128)(2,1)}), bf16[8,32,3200]{2,1,0:T(8,128)(2,1)S(1)}, u32[]{:S(2)}, u32[]{:S(2)}) async-start(bf16[8,32,3200]{2,1,0:T(8,128)(2,1)} %broadcast_in_dim.3), calls=%async_computation.2 | async-start | bytes 3276800 | tf_op jit(solution)/shard_map/all_to_all | solution.py:461
  45.7 6.3 %collective-permute-start = (bf16[1,96,6144]{2,1,0:T(8,128)(2,1)}, bf16[1,96,6144]{2,1,0:T(8,128)(2,1)S(1)}, u32[]{:S(2)}, u32[]{:S(2)}) collective-permute-start(bf16[1,96,6144]{2,1,0:T(8,128)(2,1)} %refs_2_.3), channel_id=1, source_target_pairs={{0,1},{1,0},{2,3},{3,2},{4,5},{5,4},{6,7},{7,6},{8,9},{9,8},{10,11... | collective-permute-start | bytes 3538952 | tf_op jit(solution)/shard_map/ppermute | solution.py:444
  47.6 5.1 %collective-permute-start.1 = (bf16[1,96,6144]{2,1,0:T(8,128)(2,1)}, bf16[1,96,6144]{2,1,0:T(8,128)(2,1)S(1)}, u32[]{:S(2)}, u32[]{:S(2)}) collective-permute-start(bf16[1,96,6144]{2,1,0:T(8,128)(2,1)} %refs_4_.3), channel_id=1, source_target_pairs={{0,1},{1,0},{2,3},{3,2},{4,5},{5,4},{6,7},{7,6},{8,9},{9,8},{10,11... | collective-permute-start | bytes 3538952 | tf_op jit(solution)/shard_map/ppermute | solution.py:444
  50.0 5.0 %collective-permute-start.2 = (bf16[1,96,6144]{2,1,0:T(8,128)(2,1)}, bf16[1,96,6144]{2,1,0:T(8,128)(2,1)S(1)}, u32[]{:S(2)}, u32[]{:S(2)}) collective-permute-start(bf16[1,96,6144]{2,1,0:T(8,128)(2,1)} %refs_1_.3), channel_id=1, source_target_pairs={{0,1},{1,0},{2,3},{3,2},{4,5},{5,4},{6,7},{7,6},{8,9},{9,8},{10,11... | collective-permute-start | bytes 3538952 | tf_op jit(solution)/shard_map/ppermute | solution.py:444
  52.0 1.0 %copy-start = (bf16[1,96,6144]{2,1,0:T(8,128)(2,1)}, bf16[1,96,6144]{2,1,0:T(8,128)(2,1)S(1)}, u32[]{:S(2)}) copy-start(bf16[1,96,6144]{2,1,0:T(8,128)(2,1)S(1)} %collective-permute-done.refs_0_) | copy-start | bytes 3538948
  53.0 1.0 copy-start.1

commit v7 on v5

--- a/solution.py
+++ b/solution.py
@@ -404,6 +404,33 @@
     )
 
 
+def near_sum_kernel(half_y, parts_ref, out_ref):
+    n_near, n_xh, far_rows, _ = parts_ref.shape
+    n_far, requests, _ = out_ref.shape
+    half_z = n_far // n_xh // half_y
+    for xh in range(n_xh):
+        total = parts_ref[0, xh].astype(F32)
+        for p in range(1, n_near):
+            total += parts_ref[p, xh].astype(F32)
+        for zh in range(half_z):
+            for yh in range(half_y):
+                row = (zh * half_y + yh) * requests
+                out_ref[(yh * half_z + zh) * n_xh + xh] = total[row : row + requests].astype(BF16)
+
+
+def near_sum(parts, n_far, half_y):
+    _, n_xh, far_rows, width = parts.shape
+    vmem = pl.BlockSpec(memory_space=pltpu.VMEM)
+    return pl.pallas_call(
+        functools.partial(near_sum_kernel, half_y),
+        out_shape=pltpu.VMEM((n_far, n_xh * far_rows // n_far, width), BF16),
+        in_specs=[vmem],
+        out_specs=vmem,
+        compiler_params=pltpu.CompilerParams(vmem_limit_bytes=KERNEL_VMEM),
+        name="near_sum",
+    )(in_vmem(parts))
+
+
 def on_device(
     groups,
     queries,
@@ -462,9 +489,7 @@
         requests,
     )
     partials = exchange(partials.reshape(n_near, 2, far_rows, width), near)
-    partials = jnp.sum(partials.astype(F32), axis=0).astype(BF16)
-    partials = partials.reshape(2, n_req // 2, n_exp // 4, requests, width)
-    partials = partials.transpose(2, 1, 0, 3, 4).reshape(n_far, requests, width)
+    partials = near_sum(partials, n_far, n_exp // 4)
     partials = exchange(partials, far)
     expert_sum = jnp.sum(partials.astype(F32), axis=0)
     return (stream.astype(F32) + expert_sum).astype(BF16)

time: 103 us -> 102 us (level)
  no operation moved by 1% of the time
where the time goes in v7:
time: 102 us
  blocking collectives  74.7 us (73%)
  starting transfers between devices  12.9 us (13%)
  Pallas kernels  6.03 us (6%)
  waiting for transfers between devices  4.93 us (5%)
  local copies, waits for them, and re-layouts  2.69 us (3%)
    all_to_all x3, blocking collectives, exchange(): return lax.all_to_all(x, AXES, 0, 0, axis_index_groups=groups, tiled=True)  66 us
    all_to_all x1, blocking collectives, on_device(): parts = lax.all_to_all(parts, 'ctx', 0, 0, tiled=True)  8.64 us
    all_to_all x1, starting transfers between devices, exchange(): return lax.all_to_all(x, AXES, 0, 0, axis_index_groups=groups, tiled=True)  6.66 us
    ppermute x3, starting transfers between devices, on_device(): lax.ppermute(w, 'exp', swap)  6.24 us
    pallas_call x1, Pallas kernels, expert_partials(): pl.pallas_call(functools.partial(expert_kernel, float(model_width), reque...  3.7 us
    all_to_all x1, waiting for transfers between devices, exchange(): return lax.all_to_all(x, AXES, 0, 0, axis_index_groups=groups, tiled=True)  3.26 us
  transfers between devices with their start and end apart: 4, of which 3 were waited for; matrix products, arithmetic and copies ran while one was open for 0% of the time, Pallas kernels for 0%

profile of v7, /device:TPU:9, one launch (start us, length us, event | category | flops | bytes accessed | tf_op | source)
XLA Modules:
  0.0 102.1 jit_solution(16394768194389169878)
XLA Ops:
  0.0 1.8 %attention_parts.1 = (f32[4,2,2,16,128]{4,3,2,1,0:T(8,128)S(1)}, bf16[2,2,1536]{2,1,0:T(2,128)(2,1)S(1)}, f32[2,1,1536]{2,1,0:T(1,128)S(1)}) custom-call(s32[2,2]{1,0:T(2,128)} %refs_0_.1, s32[2]{0:T(128)} %refs_1_.2, bf16[2,6144]{1,0:T(2,128)(2,1)} %refs_2_.2, bf16[1,3,64,1024]{3,2,1,0:T(8,128)(2,1)} %refs_3_.1, bf16[1,3,64,1024]{3,2,1,0:T(8,128)(2,1)} %refs_4_.2, ...), custom_call_target="tpu_custom_call" | custom-call | tf_op jit(solution)/shard_map/attention_parts/pallas_call | solution.py:188
  1.8 8.6 %all_to_all.25.parts_ref = f32[4,2,2,16,128]{4,3,2,1,0:T(8,128)S(1)} all-to-all(f32[4,2,2,16,128]{4,3,2,1,0:T(8,128)S(1)} %get-tuple-element.10), channel_id=1, replica_groups=mesh['req'=8,'ctx'=4,'exp'=16] {'ctx'}, dimensions={0} | all-to-all | bytes 262144 | tf_op jit(solution)/shard_map/all_to_all | solution.py:472
  10.5 0.3 merge_parts.1
  10.8 29.0 %all_to_all.26 = bf16[16,2,3200]{2,1,0:T(2,128)(2,1)S(1)} all-to-all(bf16[16,2,3200]{2,1,0:T(2,128)(2,1)S(1)} %get-tuple-element.14), channel_id=1, replica_groups={{0,4,8,12,128,132,136,140,256,260,264,268,384,388,392,396},{2,6,10,14,1..., dimensions={0} | all-to-all | bytes 409600 | tf_op jit(solution)/shard_map/all_to_all | solution.py:476
  39.8 0.1 reshape.13
  39.9 1.3 %broadcast_in_dim.3 = bf16[8,32,3200]{2,1,0:T(8,128)(2,1)} broadcast(bf16[32,3200]{1,0:T(8,128)(2,1)S(1)} %reshape.13), dimensions={1,2} | broadcast | bytes 1843200 | tf_op jit(solution)/shard_map/broadcast_in_dim | solution.py:480
  41.1 6.7 %all-to-all-start.2 = ((bf16[8,32,3200]{2,1,0:T(8,128)(2,1)}), bf16[8,32,3200]{2,1,0:T(8,128)(2,1)S(1)}, u32[]{:S(2)}, u32[]{:S(2)}) async-start(bf16[8,32,3200]{2,1,0:T(8,128)(2,1)} %broadcast_in_dim.3), calls=%async_computation.2 | async-start | bytes 3276800 | tf_op jit(solution)/shard_map/all_to_all | solution.py:476
  47.8 1.9 %collective-permute-start = (bf16[1,96,6144]{2,1,0:T(8,128)(2,1)}, bf16[1,96,6144]{2,1,0:T(8,128)(2,1)S(1)}, u32[]{:S(2)}, u32[]{:S(2)}) collective-permute-start(bf16[1,96,6144]{2,1,0:T(8,128)(2,1)} %refs_2_.3), channel_id=1, source_target_pairs={{0,1},{1,0},{2,3},{3,2},{4,5},{5,4},{6,7},{7,6},{8,9},{9,8},{10,11... | collective-permute-start | bytes 3538952 | tf_op jit(solution)/shard_map/ppermute | solution.py:459
  49.7 2.4 %collective-permute-start.1 = (bf16[1,96,6144]{2,1,0:T(8,128)(2,1)}, bf16[1,96,6144]{2,1,0:T(8,128)(2,1)S(1)}, u32[]{:S(2)}, u32[]{:S(2)}) collective-permute-start(bf16[1,96,6144]{2,1,0:T(8,128)(2,1)} %refs_4_.3), channel_id=1, source_target_pairs={{0,1},{1,0},{2,3},{3,2},{4,5},{5,4},{6,7},{7,6},{8,9},{9,8},{10,11... | collective-permute-start | bytes 3538952 | tf_op jit(solution)/shard_map/ppermute | solution.py:459
  52.1 1.9 %collective-permute-start.2 = (bf16[1,96,6144]{2,1,0:T(8,128)(2,1)}, bf16[1,96,6144]{2,1,0:T(8,128)(2,1)S(1)}, u32[]{:S(2)}, u32[]{:S(2)}) collective-permute-start(bf16[1,96,6144]{2,1,0:T(8,128)(2,1)} %refs_1_.3), channel_id=1, source_target_pairs={{0,1},{1,0},{2,3},{3,2},{4,5},{5,4},{6,7},{7,6},{8,9},{9,8},{10,11... | collective-permute-start | bytes 3538952 | tf_op jit(solution)/shard_map/ppermute | solution.py:459
  54.1 0.0 collective-permute-done.refs_0_
  54.1 0.0 copy-start
  54.1 0.7 collective-permute-done.1.refs_3_
  54.8 0.3 copy-done
  55.1 0.0 copy-start.1
  55.1 1.0 copy-done.1
  56.1 1.0 collective-permute-done.2.refs_5_
  57.1 3.3 %all-to-all-done.2 = bf16[8,32,3200]{2,1,0:T(8,128)(2,1)S(1)} async-done(((bf16[8,32,3200]{2,1,0:T(8,128)(2,1)}), bf16[8,32,3200]{2,1,0:T(8,128)(2,1)S(1)}, u32[]{:S(2)}, u32[]{:S(2)}) %all-to-all-start.2) | async-done | bytes 1638432 | tf_op jit(solution)/shard_map/all_to_all | solution.py:476
  60.4 3.7 %expert_partials.1 = bf16[4,2,2,32,1536]{4,3,2,1,0:T(8,128)(2,1)S(1)} custom-call(s32[16]{0:T(128)} %block_source.1, s32[16,4,16]{2,1,0:T(4,128)} %bitcast.7, f32[16,4,16]{2,1,0:T(4,128)} %bitcast.8, bf16[4,2,32,3200]{3,2,1,0:T(8,128)(2,1)S(1)} %bitcast.5, bf16[1,96,6144]{2,1,0:T(8,128)(2,1)} %copy-done, bf16[1,96,6144]{2,1,0:T(8,128)(2,1)} %refs_1_.3, ...), custom_call_target="tpu_custom_call" | custom-call | flops 905969664 | bytes 7077888 | tf_op jit(solution)/shard_map/expert_partials/pallas_call | solution.py:379
  64.1 16.8 %all_to_all.27.parts_ref = bf16[8,2,32,1536]{3,2,1,0:T(8,128)(2,1)S(1)} all-to-all(bf16[8,2,32,1536]{3,2,1,0:T(8,128)(2,1)S(1)} %bitcast.6), channel_id=1, replica_groups={{0,16,80,64,66,82,18,2},{4,20,84,68,70,86,22,6},{8,24,88,72,74,90,26,10..., dimensions={0} | all-to-all | bytes 3145728 | tf_op jit(solution)/shard_map/all_to_all | solution.py:476
  80.9 0.2 near_sum.1
  81.1 20.2 %all_to_all.28 = bf16[32,2,1536]{2,1,0:T(2,128)(2,1)S(1)} all-to-all(bf16[32,2,1536]{2,1,0:T(2,128)(2,1)S(1)} %near_sum.1), channel_id=1, replica_groups={{0,32,128,160,256,288,384,416,4,36,132,164,260,292,388,420,8,40,136,168..., dimensions={0} | all-to-all | bytes 393216 | tf_op jit(solution)/shard_map/all_to_all | solution.py:476
  101.3 0.2 convert_reduce_fusion
  101.5 0.6 add_convert_fusion
Async XLA Ops:
  41.1 19.2 %all-to-all-start.2 = ((bf16[8,32,3200]{2,1,0:T(8,128)(2,1)}), bf16[8,32,3200]{2,1,0:T(8,128)(2,1)S(1)}, u32[]{:S(2)}, u32[]{:S(2)}) async-start(bf16[8,32,3200]{2,1,0:T(8,128)(2,1)} %broadcast_in_dim.3), calls=%async_computation.2 | async-start | bytes 3276800 | tf_op jit(solution)/shard_map/all_to_all | solution.py:476
  47.8 6.3 %collective-permute-start = (bf16[1,96,6144]{2,1,0:T(8,128)(2,1)}, bf16[1,96,6144]{2,1,0:T(8,128)(2,1)S(1)}, u32[]{:S(2)}, u32[]{:S(2)}) collective-permute-start(bf16[1,96,6144]{2,1,0:T(8,128)(2,1)} %refs_2_.3), channel_id=1, source_target_pairs={{0,1},{1,0},{2,3},{3,2},{4,5},{5,4},{6,7},{7,6},{8,9},{9,8},{10,11... | collective-permute-start | bytes 3538952 | tf_op jit(solution)/shard_map/ppermute | solution.py:459
  49.7 5.1 %collective-permute-start.1 = (bf16[1,96,6144]{2,1,0:T(8,128)(2,1)}, bf16[1,96,6144]{2,1,0:T(8,128)(2,1)S(1)}, u32[]{:S(2)}, u32[]{:S(2)}) collective-permute-start(bf16[1,96,6144]{2,1,0:T(8,128)(2,1)} %refs_4_.3), channel_id=1, source_target_pairs={{0,1},{1,0},{2,3},{3,2},{4,5},{5,4},{6,7},{7,6},{8,9},{9,8},{10,11... | collective-permute-start | bytes 3538952 | tf_op jit(solution)/shard_map/ppermute | solution.py:459
  52.1 5.0 %collective-permute-start.2 = (bf16[1,96,6144]{2,1,0:T(8,128)(2,1)}, bf16[1,96,6144]{2,1,0:T(8,128)(2,1)S(1)}, u32[]{:S(2)}, u32[]{:S(2)}) collective-permute-start(bf16[1,96,6144]{2,1,0:T(8,128)(2,1)} %refs_1_.3), channel_id=1, source_target_pairs={{0,1},{1,0},{2,3},{3,2},{4,5},{5,4},{6,7},{7,6},{8,9},{9,8},{10,11... | collective-permute-start | bytes 3538952 | tf_op jit(solution)/shard_map/ppermute | solution.py:459
  54.1 1.0 %copy-start = (bf16[1,96,6144]{2,1,0:T(8,128)(2,1)}, bf16[1,96,6144]{2,1,0:T(8,128)(2,1)S(1)}, u32[]{:S(2)}) copy-start(bf16[1,96,6144]{2,1,0:T(8,128)(2,1)S(1)} %collective-permute-done.refs_0_) | copy-start | bytes 3538948
  55.1 1.0 copy-start.1
